TPU v7x, 32 devices: a whole 2x2x4 slice. The times are simulated.
32 devices in a mesh: dp: 4 (over z), fsdp: 8 (over y, x, core).
Axes of the slice: x: 2, y: 2, z: 4, core: 2. Of those that a mesh axis runs over, the one named last changes fastest.
Arguments:
- tokens: bfloat16 [64, 512, 768], P('dp', 'fsdp'), may hold values from -6 to 6
- cotangent: bfloat16 [64, 512, 768], P('dp', 'fsdp'), may hold values from -6 to 6
- key_mask: int32 [64, 512], P('dp', 'fsdp'), may hold values from 0 to 1, as said below
- seq_lengths: int32 [64], P(('dp', 'fsdp')), may hold values from 257 to 512, as said below
- block_pattern: int32 [12], replicated, may hold values from 0 to 1, as said below
- deal_order: int32 [4, 16], P('dp'), may hold values from 0 to 15, each once within a row
- qkv_weight: bfloat16 [768, 2304], P(('dp', 'fsdp')), may hold values from -0.21875 to 0.21875
- out_weight: bfloat16 [768, 768], P(('dp', 'fsdp')), may hold values from -2.5 to 2.5
- up_weight: bfloat16 [768, 3072], P(('dp', 'fsdp')), may hold values from -0.21875 to 0.21875
- down_weight: bfloat16 [3072, 768], P(('dp', 'fsdp')), may hold values from -0.109375 to 0.109375
- query_bias: bfloat16 [768], P(('dp', 'fsdp')), may hold values from -3 to 3
- value_bias: bfloat16 [768], P(('dp', 'fsdp')), may hold values from -0.29882812 to 0.29882812
- out_bias: bfloat16 [768], P(('dp', 'fsdp')), may hold values from -2 to 2
- up_bias: bfloat16 [3072], P(('dp', 'fsdp')), may hold values from -2 to 2
- down_bias: bfloat16 [768], P(('dp', 'fsdp')), may hold values from -2 to 2
- attn_gain: bfloat16 [768], P(('dp', 'fsdp')), may hold values from 0.5 to 1.5
- attn_shift: bfloat16 [768], P(('dp', 'fsdp')), may hold values from -1.1953125 to 1.1953125
- ffn_gain: bfloat16 [768], P(('dp', 'fsdp')), may hold values from 0.5 to 1.5
- ffn_shift: bfloat16 [768], P(('dp', 'fsdp')), may hold values from -1.1953125 to 1.1953125
Outputs:
- output: bfloat16 [64, 512, 768], P('dp', 'fsdp')
- grad_tokens: bfloat16 [64, 512, 768], P('dp', 'fsdp')
- grad_qkv_weight: float32 [768, 2304], P(('dp', 'fsdp'))
- grad_out_weight: float32 [768, 768], P(('dp', 'fsdp'))
- grad_up_weight: float32 [768, 3072], P(('dp', 'fsdp'))
- grad_down_weight: float32 [3072, 768], P(('dp', 'fsdp'))
- grad_query_bias: float32 [768], P(('dp', 'fsdp'))
- grad_value_bias: float32 [768], P(('dp', 'fsdp'))
- grad_out_bias: float32 [768], P(('dp', 'fsdp'))
- grad_up_bias: float32 [3072], P(('dp', 'fsdp'))
- grad_down_bias: float32 [768], P(('dp', 'fsdp'))
- grad_attn_gain: float32 [768], P(('dp', 'fsdp'))
- grad_attn_shift: float32 [768], P(('dp', 'fsdp'))
- grad_ffn_gain: float32 [768], P(('dp', 'fsdp'))
- grad_ffn_shift: float32 [768], P(('dp', 'fsdp'))
Inputs may be any that keep to these rules, and one draw needn't show every extreme that they name: `key_mask`: positions 0 and 256 of every sequence are 1. `seq_lengths`: entry d * 2 + m is the length of the sequence dealt to micro-batch m of the device with index d over dp+fsdp. In each aligned block of 16 entries one is 512. `block_pattern`: both values occur. `deal_order`: each row holds each number once.
All inputs are finite; a program needn't handle non-finite values.
Results may differ from a plain program's by a relative error of at most 0.015.
Values may be sent and summed in bfloat16 or wider, within the bound.
No kernel may reach another device: no remote copies, remote signals or barrier semaphores. Data moves between devices by JAX's collectives and lax.ppermute only.
A program may use at most 192 MiB of HBM per device.

v0:
```python
import functools

import jax
import jax.numpy as jnp
from jax import lax
from jax.experimental import pallas as pl
from jax.experimental.pallas import tpu as pltpu
from jax.sharding import PartitionSpec as P

H = 12
HD = 64
EPSILON = 1e-12
NEGATIVE = -1e30
BF = jnp.bfloat16
F32 = jnp.float32
VMEM_LIMIT = 56 * 1024 * 1024
BOTH = ("dp", "fsdp")
WEIGHT = 1


def dot(a, b):
    return jnp.dot(a, b, preferred_element_type=F32)


def dot_nt(a, b):
    return lax.dot_general(a, b, (((1,), (1,)), ((), ())), preferred_element_type=F32)


def dot_tn(a, b):
    return lax.dot_general(a, b, (((0,), (0,)), ((), ())), preferred_element_type=F32)


def whole(shape):
    return pl.BlockSpec(shape, lambda *_: (0,) * len(shape), pipeline_mode=pl.Buffered(1))


def params():
    return pltpu.CompilerParams(vmem_limit_bytes=VMEM_LIMIT)


def cost(flops, size, exps=0):
    return pl.CostEstimate(flops=int(flops * WEIGHT), bytes_accessed=int(size * WEIGHT), transcendentals=int(exps * WEIGHT))


class Pieces:
    def __init__(self, halves, spots, rows):
        self.halves, self.spots, self.rows = halves, spots, rows

    def arrays(self):
        return [a for half in self.halves for a in half]

    def specs(self):
        return [whole(a.shape) for a in self.arrays()]

    def put(self, place, refs, start, wide, out_ref):
        core, plane_at, depth_at, plane, depth = place
        each = len(refs) // 2
        for side, part in ((core, refs[:each]), (1 - core, refs[each:])):
            cols = pl.ds(pl.multiple_of(side * wide, 128), wide)
            for ref, spots in zip(part, self.spots):
                for i, (away, back) in enumerate(spots):
                    chip = lax.rem(depth_at + depth - back, depth) * plane + (plane_at ^ away)
                    rows = pl.ds(pl.multiple_of(chip * self.rows, 16), self.rows)
                    out_ref[rows, cols] = ref[i, :, start : start + wide]


def without(kernel, first, count):
    return lambda *refs: kernel(*refs[:first], *refs[first + count :])


def anywhere(arrays):
    return [pl.BlockSpec(memory_space=pl.ANY)] * len(arrays)


def tie(a, *earlier):
    return pl.pallas_call(
        lambda *refs: None,
        in_specs=anywhere((a, *earlier)),
        out_specs=pl.BlockSpec(memory_space=pl.ANY),
        out_shape=jax.ShapeDtypeStruct(a.shape, a.dtype),
        input_output_aliases={0: 0},
        compiler_params=params(),
        cost_estimate=cost(0, 0),
        name="tie",
    )(a, *earlier)


def place_of(place_ref, plane, depth):
    return place_ref[0], place_ref[1], place_ref[2], plane, depth


def load_weight(pieces, sizes, place_ref, refs, start, wide, out_ref):
    if pieces is None:
        out_ref[...] = refs[0][:, start : start + out_ref.shape[1]]
    else:
        pieces.put(place_of(place_ref, *sizes), refs, start, wide, out_ref)


def attention_kernel(pieces, sizes, n_pieces, place_ref, pattern, x_ref, b_ref, valid_ref, *refs):
    w_in, (project_ref, mixed_ref, probs_ref, w_ref) = refs[:n_pieces], refs[n_pieces:]
    width = x_ref.shape[2]
    half = x_ref.shape[1] // 2

    @pl.when(pl.program_id(0) == 0)
    def _():
        load_weight(pieces, sizes, place_ref, w_in, 0, 3 * width // 2, w_ref)

    x = x_ref[0]
    for part in range(3):
        cols = slice(part * width, (part + 1) * width)
        value = dot(x, w_ref[:, cols]) + b_ref[:, cols]
        project_ref[0, :, cols] = value.astype(BF)
    lanes = lax.broadcasted_iota(jnp.int32, (half, 2 * HD), 1) < HD

    def pair(i, carry):
        base = i * (2 * HD)
        for b in range(2):
            rows = pl.ds(b * half, half)
            q = project_ref[0, rows, pl.ds(pl.multiple_of(base, 128), 2 * HD)] * jnp.asarray(HD ** (-0.5), BF)
            outs = []
            for h in range(2):
                met = jnp.where(pattern[2 * i + h] == 1, 1 - b, b)
                off = pl.ds(pl.multiple_of(met * half, half), half)
                k = project_ref[0, off, pl.ds(pl.multiple_of(width + base, 128), 2 * HD)]
                v = project_ref[0, off, pl.ds(pl.multiple_of(2 * width + base, 128), 2 * HD)]
                own = jnp.where(lanes if h == 0 else jnp.logical_not(lanes), q, jnp.zeros_like(q))
                scores = jnp.where(valid_ref[0, met] > 0.0, dot_nt(own, k), NEGATIVE)
                e = jnp.exp(scores - jnp.max(scores, axis=-1, keepdims=True))
                p = (e * (1.0 / jnp.sum(e, axis=-1, keepdims=True))).astype(BF)
                probs_ref[0, 2 * i + h, b] = p
                outs.append(dot(p, v))
            mixed_ref[0, rows, pl.ds(pl.multiple_of(base, 128), 2 * HD)] = jnp.where(lanes, *outs).astype(BF)
        return carry

    lax.fori_loop(0, H // 2, pair, 0)


def qkv_attention(place, pattern, x3, bias, valid, pieces, sizes):
    n, length, width = x3.shape
    half = length // 2
    arrays = pieces.arrays() if isinstance(pieces, Pieces) else [pieces]
    specs = [whole(a.shape) for a in arrays]
    units = n * H * 2 * half * half
    return pl.pallas_call(
        functools.partial(
            attention_kernel, pieces if isinstance(pieces, Pieces) else None, sizes, len(arrays)
        ),
        grid_spec=pltpu.PrefetchScalarGridSpec(
            num_scalar_prefetch=2,
            grid=(n,),
            in_specs=[
                pl.BlockSpec((1, length, width), lambda s, *_: (s, 0, 0)),
                whole((1, 3 * width)),
                pl.BlockSpec((1, 2, 1, half), lambda s, *_: (s, 0, 0, 0)),
                *specs,
            ],
            out_specs=[
                pl.BlockSpec((1, length, 3 * width), lambda s, *_: (s, 0, 0)),
                pl.BlockSpec((1, length, width), lambda s, *_: (s, 0, 0)),
                pl.BlockSpec((1, H, 2, half, half), lambda s, *_: (s, 0, 0, 0, 0)),
                whole((width, 3 * width)),
            ],
        ),
        out_shape=[
            jax.ShapeDtypeStruct((n, length, 3 * width), BF),
            jax.ShapeDtypeStruct((n, length, width), BF),
            jax.ShapeDtypeStruct((n, H, 2, half, half), BF),
            jax.ShapeDtypeStruct((width, 3 * width), BF),
        ],
        compiler_params=params(),
        cost_estimate=cost(6 * n * length * width * width + 4 * units * HD * 4, 22e6, units),
        name="qkv_attention",
    )(place, pattern, x3, bias, valid, *arrays)


def norm(residual):
    centre = residual - jnp.mean(residual, axis=-1, keepdims=True)
    scale = lax.rsqrt(jnp.mean(centre * centre, axis=-1, keepdims=True) + EPSILON)
    return centre * scale, scale


def norm_back(normed, scale, gained):
    inner = jnp.mean(gained * normed, axis=-1, keepdims=True)
    return scale * (gained - jnp.mean(gained, axis=-1, keepdims=True) - normed * inner)


def up_kernel(chunk, mixed_ref, x_ref, vec_ref, up_b_ref, out_w_ref, *refs):
    up_w, (normed_ref, scale_ref, low_ref, act_ref, slope_ref) = refs[:-5], refs[-5:]
    width = x_ref.shape[1]
    normed, scale = norm(x_ref[...].astype(F32) + dot(mixed_ref[...], out_w_ref[...]) + vec_ref[0:1])
    normed_ref[...] = normed
    scale_ref[...] = scale
    low = (normed * vec_ref[1:2] + vec_ref[2:3]).astype(BF)
    low_ref[...] = low
    for j, up_w_ref in enumerate(up_w):
        for start in range(0, width, chunk):
            cols = slice(j * width + start, j * width + start + chunk)
            u = dot(low, up_w_ref[:, start : start + chunk]) + up_b_ref[:, cols]
            phi = 0.5 + 0.5 * lax.erf(u * (2.0 ** -0.5))
            density = jnp.exp(-0.5 * u * u) * 0.3989422804014327
            act_ref[:, cols] = (u * phi).astype(BF)
            slope_ref[:, cols] = (phi + u * density).astype(BF)


def rows_of(tile, width):
    return pl.BlockSpec((tile, width), lambda i, *_: (i, 0))


def out_up(mixed, x, vecs, up_b, out_w, up_w, tile=256, chunk=384):
    rows, width = x.shape
    wide = up_b.shape[1]
    return pl.pallas_call(
        functools.partial(up_kernel, chunk),
        grid=(rows // tile,),
        in_specs=[
            rows_of(tile, width),
            rows_of(tile, width),
            *[whole(a.shape) for a in (vecs, up_b, out_w, *up_w)],
        ],
        out_specs=[
            rows_of(tile, width),
            rows_of(tile, 1),
            rows_of(tile, width),
            rows_of(tile, wide),
            rows_of(tile, wide),
        ],
        out_shape=[
            jax.ShapeDtypeStruct((rows, width), F32),
            jax.ShapeDtypeStruct((rows, 1), F32),
            jax.ShapeDtypeStruct((rows, width), BF),
            jax.ShapeDtypeStruct((rows, wide), BF),
            jax.ShapeDtypeStruct((rows, wide), BF),
        ],
        compiler_params=params(),
        cost_estimate=cost(2 * rows * width * (width + wide), 38e6, rows * wide),
        name="out_up",
    )(mixed, x, vecs, up_b, out_w, *up_w)


def down_kernel(act_ref, slope_ref, normed_ref, g_ref, vec_ref, w_ref, *refs):
    out_ref, two_ref, down_low_ref, up_low_ref, sums_ref, up_sum_ref = refs
    width = normed_ref.shape[1]

    @pl.when(pl.program_id(0) == 0)
    def _():
        sums_ref[...] = jnp.zeros_like(sums_ref)
        up_sum_ref[...] = jnp.zeros_like(up_sum_ref)

    hidden = normed_ref[...] * vec_ref[0:1] + vec_ref[1:2]
    normed, scale = norm(hidden + dot(act_ref[...], w_ref[...]) + vec_ref[2:3])
    out_ref[...] = (normed * vec_ref[3:4] + vec_ref[4:5]).astype(BF).reshape(out_ref.shape)
    g = g_ref[...].reshape(normed_ref.shape).astype(F32)
    two = norm_back(normed, scale, g * vec_ref[3:4])
    two_ref[...] = two
    low = two.astype(BF)
    down_low_ref[...] = low
    sums_ref[0:1] += jnp.sum(g * normed, axis=0, keepdims=True)
    sums_ref[1:2] += jnp.sum(g, axis=0, keepdims=True)
    sums_ref[2:3] += jnp.sum(low.astype(F32), axis=0, keepdims=True)
    for start in range(0, w_ref.shape[0], width):
        cols = slice(start, start + width)
        up_low = (dot_nt(low, w_ref[cols, :]) * slope_ref[:, cols].astype(F32)).astype(BF)
        up_low_ref[:, cols] = up_low
        up_sum_ref[:, cols] += jnp.sum(up_low.astype(F32), axis=0, keepdims=True)


def given(tile, piece, length, width):
    return pl.BlockSpec(
        (tile // piece, 1, piece, width), lambda i, *_: (lax.rem(i, length // tile), i // (length // tile), 0, 0)
    )


def down_and_back(active, slope, normed, g, vecs, down_w, piece, length, tile=256):
    rows, width = normed.shape
    wide = active.shape[1]
    return pl.pallas_call(
        down_kernel,
        grid=(rows // tile,),
        in_specs=[
            rows_of(tile, wide),
            rows_of(tile, wide),
            rows_of(tile, width),
            given(tile, piece, length, width),
            whole(vecs.shape),
            whole(down_w.shape),
        ],
        out_specs=[
            given(tile, piece, length, width),
            rows_of(tile, width),
            rows_of(tile, width),
            rows_of(tile, wide),
            whole((8, width)),
            whole((1, wide)),
        ],
        out_shape=[
            jax.ShapeDtypeStruct((length // piece, rows // length, piece, width), BF),
            jax.ShapeDtypeStruct((rows, width), F32),
            jax.ShapeDtypeStruct((rows, width), BF),
            jax.ShapeDtypeStruct((rows, wide), BF),
            jax.ShapeDtypeStruct((8, width), F32),
            jax.ShapeDtypeStruct((1, wide), F32),
        ],
        compiler_params=params(),
        cost_estimate=cost(4 * rows * width * wide, 38e6),
        name="down_and_back",
    )(active, slope, normed, g, vecs, down_w)


def up_back_kernel(up_low_ref, two_ref, normed_ref, scale_ref, gain_ref, out_w_ref, *refs):
    up_w, (one_ref, low_ref, mixed_ref, sums_ref) = refs[:-4], refs[-4:]
    width = two_ref.shape[1]

    @pl.when(pl.program_id(0) == 0)
    def _():
        sums_ref[...] = jnp.zeros_like(sums_ref)

    hidden = two_ref[...]
    for j, up_w_ref in enumerate(up_w):
        hidden = hidden + dot_nt(up_low_ref[:, j * width : (j + 1) * width], up_w_ref[...])
    normed = normed_ref[...]
    one = norm_back(normed, scale_ref[...], hidden * gain_ref[...])
    one_ref[...] = one
    low = one.astype(BF)
    low_ref[...] = low
    mixed_ref[...] = dot_nt(low, out_w_ref[...]).astype(BF)
    sums_ref[0:1] += jnp.sum(hidden * normed, axis=0, keepdims=True)
    sums_ref[1:2] += jnp.sum(hidden, axis=0, keepdims=True)
    sums_ref[2:3] += jnp.sum(low.astype(F32), axis=0, keepdims=True)


def up_back(up_low, two, normed, scale, gain, out_w, up_w, earlier, tile=256):
    rows, wide = up_low.shape
    width = two.shape[1]
    narrow = rows_of(tile, width)
    return pl.pallas_call(
        without(up_back_kernel, 6 + len(up_w), len(earlier)),
        grid=(rows // tile,),
        in_specs=[
            rows_of(tile, wide),
            narrow,
            narrow,
            rows_of(tile, 1),
            *[whole(a.shape) for a in (gain, out_w, *up_w)],
            *anywhere(earlier),
        ],
        out_specs=[narrow, narrow, narrow, whole((8, width))],
        out_shape=[
            jax.ShapeDtypeStruct((rows, width), F32),
            jax.ShapeDtypeStruct((rows, width), BF),
            jax.ShapeDtypeStruct((rows, width), BF),
            jax.ShapeDtypeStruct((8, width), F32),
        ],
        compiler_params=params(),
        cost_estimate=cost(2 * rows * width * (wide + width), 28e6),
        name="up_back",
    )(up_low, two, normed, scale, gain, out_w, *up_w, *earlier)


def attention_back_kernel(pattern, project_ref, probs_ref, g_ref, out_ref, sums_ref):
    width = g_ref.shape[2]
    half = g_ref.shape[1] // 2
    scale = HD ** (-0.5)
    lanes = lax.broadcasted_iota(jnp.int32, (half, 2 * HD), 1) < HD

    def pair(i, carry):
        base = i * (2 * HD)
        q_cols, k_cols, v_cols = (pl.ds(pl.multiple_of(j * width + base, 128), 2 * HD) for j in range(3))
        for b in range(2):
            rows = pl.ds(b * half, half)
            q = project_ref[0, rows, q_cols]
            g = g_ref[0, rows, q_cols]
            grads = []
            for h in range(2):
                mine = lanes if h == 0 else jnp.logical_not(lanes)
                met = jnp.where(pattern[2 * i + h] == 1, 1 - b, b)
                off = pl.ds(pl.multiple_of(met * half, half), half)
                k = project_ref[0, off, k_cols]
                v = project_ref[0, off, v_cols]
                p = probs_ref[0, 2 * i + h, b]
                wide = p.astype(F32)
                gp = dot_nt(jnp.where(mine, g, jnp.zeros_like(g)), v)
                inner = jnp.sum(wide * gp, axis=-1, keepdims=True)
                gs = (wide * (gp - inner)).astype(BF)
                grads.append(dot(gs, k))
                dk = (dot_tn(gs, q) * scale).astype(BF)
                dv = dot_tn(p, g).astype(BF)
                out_ref[0, off, k_cols] = jnp.where(mine, dk, out_ref[0, off, k_cols])
                out_ref[0, off, v_cols] = jnp.where(mine, dv, out_ref[0, off, v_cols])
            out_ref[0, rows, q_cols] = (jnp.where(lanes, *grads) * scale).astype(BF)
        return carry

    lax.fori_loop(0, H // 2, pair, 0)

    @pl.when(pl.program_id(0) == 0)
    def _():
        sums_ref[...] = jnp.zeros_like(sums_ref)

    sums_ref[...] += jnp.sum(out_ref[0].astype(F32), axis=0, keepdims=True)


def attention_back(project, probs, grad_mixed, pattern, earlier):
    n, length, width3 = project.shape
    width = width3 // 3
    half = length // 2
    units = n * H * 2 * half * half
    return pl.pallas_call(
        without(attention_back_kernel, 4, len(earlier)),
        grid_spec=pltpu.PrefetchScalarGridSpec(
            num_scalar_prefetch=1,
            grid=(n,),
            in_specs=[
                pl.BlockSpec((1, length, width3), lambda s, *_: (s, 0, 0)),
                pl.BlockSpec((1, H, 2, half, half), lambda s, *_: (s, 0, 0, 0, 0)),
                pl.BlockSpec((1, length, width), lambda s, *_: (s, 0, 0)),
                *anywhere(earlier),
            ],
            out_specs=[
                pl.BlockSpec((1, length, width3), lambda s, *_: (s, 0, 0)),
                whole((1, width3)),
            ],
        ),
        out_shape=[
            jax.ShapeDtypeStruct((n, length, width3), BF),
            jax.ShapeDtypeStruct((1, width3), F32),
        ],
        compiler_params=params(),
        cost_estimate=cost(8 * units * HD * 4, 20e6),
        name="attention_back",
    )(pattern, project, probs, grad_mixed, *earlier)


def tokens_kernel(one_ref, project_ref, w_ref, out_ref):
    out_ref[...] = (one_ref[...] + dot_nt(project_ref[...], w_ref[...])).astype(BF).reshape(out_ref.shape)


def tokens_back(one, grad_project, weight, piece, length, earlier, tile=256):
    rows, width = one.shape
    return pl.pallas_call(
        without(tokens_kernel, 3, len(earlier)),
        grid=(rows // tile,),
        in_specs=[
            rows_of(tile, width),
            rows_of(tile, grad_project.shape[1]),
            whole(weight.shape),
            *anywhere(earlier),
        ],
        out_specs=given(tile, piece, length, width),
        out_shape=jax.ShapeDtypeStruct((length // piece, rows // length, piece, width), BF),
        compiler_params=params(),
        cost_estimate=cost(2 * rows * width * grad_project.shape[1], 14e6),
        name="tokens_back",
    )(one, grad_project, weight, *earlier)


def core_swap(a):
    return lax.ppermute(a, "fsdp", [(i, i ^ 1) for i in range(lax.axis_size("fsdp"))])


def z_shift(a, k):
    n = lax.axis_size("dp")
    return lax.ppermute(a, "dp", [(i, (i + k) % n) for i in range(n)])


def z_pieces(a):
    return [a] + [z_shift(a, k) for k in range(1, lax.axis_size("dp"))]


def hop(a, away):
    return lax.ppermute(a, "fsdp", [(i, i ^ (2 * away)) for i in range(lax.axis_size("fsdp"))])


def plane_pieces(a):
    return [a] + [hop(a, away) for away in (1, 2, 3)]


def z_parts(a):
    n = lax.axis_size("dp")
    me = lax.axis_index("dp")
    return [lax.dynamic_index_in_dim(a, lax.rem(me + k, n), 0, False) for k in range(n)]


def z_scatter(parts):
    return [parts[0]] + [z_shift(a, k) for k, a in enumerate(parts) if k]


def total(parts):
    value = parts[0].astype(F32)
    for part in parts[1:]:
        value = value + part.astype(F32)
    return value


def after(a, *earlier):
    return lax.optimization_barrier((a, *earlier))[0]


def plane_exchange(a):
    size = lax.axis_size("fsdp")
    groups = [list(range(c, size, 2)) for c in range(2)]
    return lax.all_to_all(a, "fsdp", 0, 0, tiled=True, axis_index_groups=groups)


def by_plane(part):
    depth, plane = lax.axis_size("dp"), lax.axis_size("fsdp") // 2
    return jnp.transpose(part.reshape(depth, plane, -1, part.shape[1]), (1, 0, 2, 3))


def core_order(core, own, other, axis):
    return jnp.where(core == 0, jnp.concatenate([own, other], axis), jnp.concatenate([other, own], axis))


def half_of(a, which):
    wide = a.shape[1] // 2
    return lax.dynamic_slice_in_dim(a, which * wide, wide, 1)


def with_other_core(mine, spots, rows):
    return Pieces([mine, [core_swap(a) for a in mine]], spots, rows)


def plane_spots(depth):
    return [[(away, k) for k in range(depth)] for away in range(4)]


def finish(core, total):
    rows = total.shape[0] // 2
    own = lax.dynamic_slice_in_dim(total, core * rows, rows, 0)
    other = core_swap(lax.dynamic_slice_in_dim(total, (1 - core) * rows, rows, 0))
    return core_order(core, own, other, 1)


def summed(a):
    return jnp.sum(a.astype(F32), axis=0)


def hops(parts):
    return [parts[0]] + [hop(a, away) for away, a in enumerate(parts) if away]


def local(tokens, cotangent, key_mask, seq_lengths, block_pattern, deal_order, *shards):
    qkv_s, out_s, up_s, down_s = shards[:4]
    fsdp, depth = lax.axis_size("fsdp"), lax.axis_size("dp")
    devices, plane = fsdp * depth, fsdp // 2
    me = lax.axis_index("fsdp")
    core = lax.rem(me, 2)
    count, piece, width = tokens.shape
    per = count // fsdp
    length = piece * fsdp
    flat = (per * length, width)
    rows = 2 * qkv_s.shape[0]
    fast = rows % 16 == 0 and plane == 4 and depth % 2 == 0
    place = jnp.stack([core, me // 2, lax.axis_index("dp")]).astype(jnp.int32)
    sizes = (plane, depth)

    def deal(a):
        return lax.all_to_all(a, "fsdp", split_axis=0, concat_axis=1, tiled=True)

    def give(a):
        return lax.all_to_all(a, "fsdp", 0, 0, tiled=True).reshape(count, piece, width)

    slot = -(-shards[7].shape[0] // 128) * 128
    vectors = jnp.stack([jnp.pad(v.astype(F32), (0, slot - v.shape[0])) for v in shards[4:]]).reshape(-1)
    n_vec = vectors.shape[0]
    marks = key_mask.reshape(fsdp, per * piece)
    own = jnp.concatenate([vectors, seq_lengths.astype(F32)])
    notes = jnp.concatenate([marks.astype(F32), jnp.broadcast_to(own[None], (fsdp, own.shape[0]))], 1)
    notes = lax.all_to_all(notes, "fsdp", 0, 0, tiled=True)
    marks = notes[:, : per * piece].reshape(fsdp, per, piece).transpose(1, 0, 2).reshape(per, length)
    by_slot = notes[:, per * piece + n_vec :].T.reshape(-1).astype(jnp.int32)
    own_ids = me * per + jnp.arange(per, dtype=jnp.int32)
    own_lengths = jnp.sum(jnp.where(deal_order[0][None, :] == own_ids[:, None], by_slot[None, :], 0), axis=1)
    positions = jnp.arange(length, dtype=jnp.int32)
    valid = ((marks > 0.5) & (positions[None, :] < own_lengths[:, None])).astype(F32)
    valid = valid.reshape(per, 2, 1, length // 2)
    every = notes[:, per * piece : per * piece + n_vec].astype(BF)
    x3 = deal(after(tokens, notes))
    folds = up_s.shape[1] // width
    own = jnp.concatenate([out_s] + [up_s[:, j * width : (j + 1) * width] for j in range(folds)] + [down_s], 0)
    ffn_w = lax.all_gather(own[None], BOTH, axis=0, tiled=True)
    n = out_s.shape[0]
    out_w, *up_w = (ffn_w[:, j * n : (j + 1) * n].reshape(width, width) for j in range(1 + folds))
    down_w = ffn_w[:, (1 + folds) * n :].reshape(-1, width)
    if fast:
        chip = core_order(core, half_of(qkv_s, core), core_swap(half_of(qkv_s, 1 - core)), 0)
        every = jnp.pad(every, ((0, 8), (0, chip.shape[1] - n_vec)))
        first = z_pieces(jnp.concatenate([chip, every], 0))
        every = jnp.stack([a[rows : rows + fsdp, :n_vec] for a in first], 1)
        first = plane_pieces(jnp.stack([a[:rows] for a in first]))
        qkv_w = with_other_core(first, plane_spots(depth), rows)
        every = jnp.concatenate([every[:, :1], every[:, :0:-1]], 1)
        turn = lax.rem(depth - place[2], depth)
        every = lax.dynamic_slice_in_dim(jnp.concatenate([every, every], 1), turn, depth, 1)
        every = jnp.transpose(every, (1, 0, 2)).reshape(devices, n_vec)
    else:
        qkv_w = lax.all_gather(qkv_s, BOTH, axis=0, tiled=True)
        every = lax.all_gather(every, "dp", axis=0, tiled=True)
    every = every.astype(F32)
    lens = [s.shape[0] for s in shards[4:]]
    starts = [sum(lens[:i]) for i in range(len(lens))]
    query_b, value_b, out_b, up_b, down_b, attn_gain, attn_shift, ffn_gain, ffn_shift = (
        every[:, i * slot : i * slot + n].reshape(1, -1) for i, n in enumerate(lens)
    )


    bias_all = jnp.concatenate([query_b, jnp.zeros_like(query_b), value_b], 1)
    project, mixed, probs, qkv_w = qkv_attention(place, block_pattern, x3, bias_all, valid, qkv_w, sizes)
    mixed = mixed.reshape(flat)
    x = x3.reshape(flat)
    g = lax.all_to_all(tie(cotangent, mixed), "fsdp", 0, 0, tiled=True)
    normed, scale, hidden_low, active, slope = out_up(
        mixed, x, jnp.concatenate([out_b, attn_gain, attn_shift]), up_b, out_w, up_w
    )
    g = tie(g, active).reshape(fsdp, per, piece, width)
    vecs = jnp.concatenate([attn_gain, attn_shift, down_b, ffn_gain, ffn_shift])
    output, grad_two, down_low, up_low, ffn_sums, grad_up_b = down_and_back(
        active, slope, normed, g, vecs, down_w, piece, length
    )
    if not fast:
        output = give(output)

    up_gate = attention_gate = tokens_gate = ()
    if fast:
        down_sent = dot_tn(active, half_of(down_low, 1 - core)).astype(BF)
        up_sent = dot_tn(hidden_low, half_of(up_low, 1 - core)).astype(BF)
        down_part = total([dot_tn(active, half_of(down_low, core)), core_swap(down_sent)]).astype(BF)
        down_part = by_plane(down_part)
        up_kept = total([dot_tn(hidden_low, half_of(up_low, core)), core_swap(up_sent)]).astype(BF)
        up_gate = (down_part, up_kept)
        down_part = plane_exchange(down_part)
    grad_one, out_low, grad_mixed, attn_sums = up_back(
        up_low, grad_two, normed, scale, attn_gain, out_w, up_w, up_gate
    )
    early = jnp.concatenate([attn_sums, ffn_sums], 0)
    early = jnp.transpose(early.reshape(early.shape[0], devices, -1), (1, 0, 2)).reshape(devices, -1)
    early = jnp.concatenate([early, grad_up_b.reshape(devices, -1)], 1)
    if fast:
        early = (early + core_swap(early)).reshape(depth, plane, 2, -1).astype(BF)
        early = jnp.pad(early, ((0, 0), (0, 0), (0, 0), (0, 3 * width // 2 - early.shape[3])))
        out_sent = dot_tn(mixed, half_of(out_low, 1 - core)).astype(BF)
        out_kept = total([dot_tn(mixed, half_of(out_low, core)), core_swap(out_sent)]).astype(BF)
        up_part = by_plane(jnp.concatenate([up_kept, out_kept], 1))
        down_part = summed(tie(down_part, up_part)).astype(BF)
        down_part = jnp.concatenate([down_part[:, i * rows : (i + 1) * rows] for i in range(4)], 2)
        up_part = tie(up_part, down_part)
        attention_gate = (early, up_part, down_part)
        up_part = plane_exchange(up_part)
    grad_project, bias_sums = attention_back(
        project, probs, grad_mixed.reshape(per, length, width), block_pattern, attention_gate
    )
    grad_project = grad_project.reshape(per * length, 3 * width)
    if fast:
        up_part = summed(tie(up_part, grad_project)).astype(BF)
        output = give(tie(output, up_part))
        up_part = z_parts(jnp.concatenate([up_part, tie(down_part, bias_sums)], 2))
        grad_project = tie(grad_project, *up_part)
        qkv_sent = dot_tn(x, half_of(grad_project, 1 - core)).astype(BF)
        biases = (bias_sums + core_swap(bias_sums)).reshape(2, -1).astype(BF)
        qkv_kept = total([dot_tn(x, half_of(grad_project, core)), core_swap(qkv_sent)]).astype(BF)
        wide = qkv_kept.shape[1]
        biases = jnp.pad(biases, ((0, 4), (0, 0)))
        extra = jnp.concatenate([early, jnp.broadcast_to(biases, (depth, plane, *biases.shape))], 2)
        qkv_part = jnp.concatenate([qkv_kept.reshape(depth, plane, rows, wide), extra], 2)
        qkv_part = [lax.dynamic_index_in_dim(qkv_part, place[1] ^ away, 1, False) for away in range(plane)]
        up_part = z_scatter(up_part)
        tokens_gate = tuple(qkv_part)
        qkv_part = hops(qkv_part)
    grad_tokens = tokens_back(grad_one, grad_project, qkv_w, piece, length, tokens_gate)
    if fast:
        cut = up_s.shape[1] // 2
        up_part = total([up_part[0]] + [tie(a, grad_tokens) for a in up_part[1:]])
        down_part = up_part[:, cut + width // 2 :].reshape(rows, 4, width // 2)
        down_part = jnp.transpose(down_part, (1, 0, 2)).reshape(4 * rows, width // 2)
        grad_down_w = finish(core, down_part)
        grad_up_w = finish(core, up_part[:, :cut])
        grad_out_w = finish(core, up_part[:, cut : cut + width // 2])
        qkv_part = [qkv_part[0]] + [tie(a, grad_tokens) for a in qkv_part[1:]]
        output = tie(output, grad_tokens)
        grad_tokens = give(tie(grad_tokens, output))
        last = total(z_scatter(z_parts(total(qkv_part).astype(BF))))
        grad_qkv_w = finish(core, last[:rows])
        biases = last[rows + 2 : rows + 4].reshape(-1)
        at = (place[2] * fsdp + me) * lens[0]
        vector = jnp.concatenate(
            [
                lax.dynamic_slice_in_dim(biases, at, lens[0], 0),
                lax.dynamic_slice_in_dim(biases, at + 2 * width, lens[0], 0),
                lax.dynamic_index_in_dim(last[rows : rows + 2], core, 0, False)[: 16 * lens[0] + lens[3]],
            ]
        )
    else:
        grad_tokens = give(grad_tokens)
        late = jnp.concatenate([bias_sums[:, :width], bias_sums[:, 2 * width :]], 0)
        late = jnp.transpose(late.reshape(2, devices, -1), (1, 0, 2)).reshape(devices, -1)
        laid = jnp.concatenate([late, early], 1)
        grads = (dot_tn(x, grad_project), dot_tn(mixed, out_low), dot_tn(hidden_low, up_low))
        grads = (*grads, dot_tn(active, down_low), laid)
        grad_qkv_w, grad_out_w, grad_up_w, grad_down_w, vector = (
            lax.psum_scatter(w.astype(BF), BOTH, scatter_dimension=0, tiled=True).astype(F32) for w in grads
        )
        vector = vector.reshape(-1)
    n = lens[0]
    spots = (0, 1, 4, 18, 12, 2, 3, 10, 11)
    vectors_out = [vector[i * n : i * n + size] for i, size in zip(spots, lens)]
    return (output, grad_tokens, grad_qkv_w, grad_out_w, grad_up_w, grad_down_w, *vectors_out)


def solution(mesh):
    rows = P(BOTH, None)
    vec = P(BOTH)
    in_specs = (
        P("dp", "fsdp", None),
        P("dp", "fsdp", None),
        P("dp", "fsdp"),
        vec,
        P(),
        P("dp", None),
        *([rows] * 4),
        *([vec] * 9),
    )
    out_specs = (P("dp", "fsdp", None), P("dp", "fsdp", None), *([rows] * 4), *([vec] * 9))
    return jax.shard_map(local, mesh=mesh, in_specs=in_specs, out_specs=out_specs, check_vma=False)
```

profile of v0, /device:TPU:0, one launch (start us, length us, event | category | flops | bytes accessed | tf_op | source)
XLA Modules:
  0.0 359.3 jit_solution(12398633708876963503)
XLA Ops:
  7.4 2.9 copy.128.refs_0_
  12.7 4.8 %all-to-all-start = ((f32[8,1,1282]{2,1,0:T(1,128)}), f32[8,1,1282]{2,1,0:T(1,128)S(1)}, u32[]{:S(2)}, u32[]{:S(2)}) async-start(f32[8,1,1282]{2,1,0:T(1,128)} %all_to_all.36), calls=%async_computation | async-start | bytes 90112 | tf_op jit(solution)/shard_map/all_to_all | solution.py:567
  18.1 4.3 %all-to-all-done = f32[8,1,1282]{2,1,0:T(1,128)S(1)} async-done(((f32[8,1,1282]{2,1,0:T(1,128)}), f32[8,1,1282]{2,1,0:T(1,128)S(1)}, u32[]{:S(2)}, u32[]{:S(2)}) %all-to-all-start) | async-done | bytes 41056 | tf_op jit(solution)/shard_map/all_to_all | solution.py:567
  22.8 3.6 all-to-all-start.1
  27.3 3.7 %collective-permute-start.3 = (bf16[64,1152]{1,0:T(8,128)(2,1)S(1)}, bf16[64,1152]{1,0:T(8,128)(2,1)S(1)}, u32[]{:S(2)}, u32[]{:S(2)}) collective-permute-start(bf16[64,1152]{1,0:T(8,128)(2,1)S(1)} %fusion.29), channel_id=1, source_target_pairs={{0,24},{8,0},{16,8},{24,16},{1,25},{9,1},{17,9},{25,17},{2,26},{10... | collective-permute-start | bytes 442376 | tf_op jit(solution)/shard_map/ppermute | solution.py:461
  32.0 5.2 %collective-permute-done.3 = bf16[64,1152]{1,0:T(8,128)(2,1)S(1)} collective-permute-done((bf16[64,1152]{1,0:T(8,128)(2,1)S(1)}, bf16[64,1152]{1,0:T(8,128)(2,1)S(1)}, u32[]{:S(2)}, u32[]{:S(2)}) %collective-permute-start.3) | collective-permute-done | bytes 147488 | tf_op jit(solution)/shard_map/ppermute | solution.py:461
  37.2 10.5 %collective-permute-done.2 = bf16[64,1152]{1,0:T(8,128)(2,1)S(1)} collective-permute-done((bf16[64,1152]{1,0:T(8,128)(2,1)S(1)}, bf16[64,1152]{1,0:T(8,128)(2,1)S(1)}, u32[]{:S(2)}, u32[]{:S(2)}) %collective-permute-start.2) | collective-permute-done | bytes 147488 | tf_op jit(solution)/shard_map/ppermute | solution.py:461
  51.5 18.7 %collective-permute-done.6.refs_3_ = bf16[4,48,1152]{2,1,0:T(8,128)(2,1)S(1)} collective-permute-done((bf16[4,48,1152]{2,1,0:T(8,128)(2,1)S(1)}, bf16[4,48,1152]{2,1,0:T(8,128)(2,1)S(1)}, u32[]{:S(2)}, u32[]{:S(2)}) %collective-permute-start.6) | collective-permute-done | bytes 442400 | tf_op jit(solution)/shard_map/ppermute | solution.py:469
  70.3 8.3 %collective-permute-done.4.refs_1_ = bf16[4,48,1152]{2,1,0:T(8,128)(2,1)S(1)} collective-permute-done((bf16[4,48,1152]{2,1,0:T(8,128)(2,1)S(1)}, bf16[4,48,1152]{2,1,0:T(8,128)(2,1)S(1)}, u32[]{:S(2)}, u32[]{:S(2)}) %collective-permute-start.4) | collective-permute-done | bytes 442400 | tf_op jit(solution)/shard_map/ppermute | solution.py:469
  81.4 25.2 %qkv_attention.1 = (bf16[2,512,2304]{2,1,0:T(8,128)(2,1)}, bf16[2,512,768]{2,1,0:T(8,128)(2,1)}, bf16[2,12,2,256,256]{4,3,2,1,0:T(8,128)(2,1)}, bf16[768,2304]{1,0:T(8,128)(2,1)}) custom-call(s32[3]{0:T(128)} %pad_add_fusion.place_ref, s32[12]{0:T(128)} %refs_0_.2, bf16[2,512,768]{2,1,0:T(8,128)(2,1)} %bitcast.143, f32[1,2304]{1,0:T(1,128)} %fusion.41.b_ref, ...), custom_call_target="tpu_custom_call" | custom-call | flops 6845104128 | bytes 22000000 | tf_op jit(solution)/shard_map/qkv_attention/pallas_call | solution.py:144
  106.5 4.1 %all-to-all-start.2 = ((bf16[16,64,768]{2,1,0:T(8,128)(2,1)}), bf16[16,64,768]{2,1,0:T(8,128)(2,1)S(1)}, u32[]{:S(2)}, u32[]{:S(2)}) async-start(bf16[16,64,768]{2,1,0:T(8,128)(2,1)} %tie.16), calls=%async_computation.2 | async-start | bytes 3145728 | tf_op jit(solution)/shard_map/all_to_all | solution.py:609
  113.2 4.8 %all-gather.3.cloned.1.call-done = bf16[6912,768]{1,0:T(8,128)(2,1)} async-done(((bf16[216,768]{1,0:T(8,128)(2,1)}), bf16[6912,768]{1,0:T(8,128)(2,1)}) %all-gather.3.cloned.1.call-update) | async-done | bytes 10616848 | tf_op jit(solution)/shard_map/all_gather | solution.py:579
  118.0 4.8 %slice.242 = bf16[32,96,768]{2,1,0:T(8,128)(2,1)} slice(bf16[32,216,768]{2,1,0:T(8,128)(2,1)} %bitcast.135), slice={[0:32], [120:216], [0:768]} | slice | bytes 9437184 | tf_op jit(solution)/shard_map/slice | solution.py:582
  122.8 5.4 %fusion.45 = (bf16[32,24,768]{2,1,0:T(8,128)(2,1)}, bf16[32,24,768]{2,1,0:T(8,128)(2,1)}, bf16[32,24,768]{2,1,0:T(8,128)(2,1)}, bf16[32,24,768]{2,1,0:T(8,128)(2,1)}, bf16[32,24,768]{2,1,0:T(8,128)(2,1)}) fusion(bf16[32,216,768]{2,1,0:T(8,128)(2,1)} %bitcast.136), kind=kLoop, calls=%fused_computation.141 | loop fusion | bytes 11796480 | tf_op jit(solution)/shard_map/slice | solution.py:581
  128.1 15.7 %out_up.1 = (f32[1024,768]{1,0:T(8,128)}, f32[1024,1]{1,0:T(8,128)}, bf16[1024,768]{1,0:T(8,128)(2,1)}, bf16[1024,3072]{1,0:T(8,128)(2,1)}, bf16[1024,3072]{1,0:T(8,128)(2,1)}) custom-call(bf16[1024,768]{1,0:T(8,128)(2,1)} %bitcast.160, bf16[1024,768]{1,0:T(8,128)(2,1)} %bitcast.144, f32[3,768]{1,0:T(4,128)} %pad_maximum_fusion.7.vec_ref, ...), custom_call_target="tpu_custom_call" | custom-call | flops 6039797760 | bytes 38000000 | tf_op jit(solution)/shard_map/out_up/pallas_call | solution.py:212
  145.0 22.6 %down_and_back.1 = (bf16[8,2,64,768]{3,2,1,0:T(8,128)(2,1)}, f32[1024,768]{1,0:T(8,128)}, bf16[1024,768]{1,0:T(8,128)(2,1)}, bf16[1024,3072]{1,0:T(8,128)(2,1)}, f32[8,768]{1,0:T(8,128)}, /*index=5*/f32[1,3072]{1,0:T(1,128)}) custom-call(bf16[1024,3072]{1,0:T(8,128)(2,1)} %get-tuple-element.39.refs_1_.act_ref, ...), custom_call_target="tpu_custom_call" | custom-call | flops 9663676416 | bytes 38000000 | tf_op jit(solution)/shard_map/down_and_back/pallas_call | solution.py:276
  167.6 6.1 %convolution_convert_fusion = bf16[3072,384]{1,0:T(8,128)(2,1)} fusion(bf16[1024,3072]{1,0:T(8,128)(2,1)S(1)} %bitcast.139, bf16[1024,768]{1,0:T(8,128)(2,1)} %get-tuple-element.47, s32[]{:T(128)S(6)} %select_n.154), kind=kOutput, calls=%fused_computation.2 | convolution fusion | flops 2417098752 | bytes 9437188 | tf_op jit(solution)/shard_map/dot_general | solution.py:30
  174.1 6.4 %convolution_convert_fusion.1 = bf16[768,1536]{1,0:T(8,128)(2,1)} fusion(bf16[1024,768]{1,0:T(8,128)(2,1)} %get-tuple-element.43, bf16[1024,3072]{1,0:T(8,128)(2,1)} %get-tuple-element.44.refs_0_, s32[]{:T(128)S(6)} %select_n.152), kind=kOutput, calls=%fused_computation.4 | convolution fusion | flops 2417098752 | bytes 7077892 | tf_op jit(solution)/shard_map/dot_general | solution.py:30
  180.8 6.4 %add_convert_fusion = bf16[3072,384]{1,0:T(8,128)(2,1)S(1)} fusion(bf16[3072,384]{1,0:T(8,128)(2,1)S(1)} %collective-permute-done.12, bf16[1024,3072]{1,0:T(8,128)(2,1)} %get-tuple-element.39.refs_1_.act_ref, bf16[1024,768]{1,0:T(8,128)(2,1)} %get-tuple-element.47, s32[]{:T(128)S(6)} %select_n.153), kind=kOutput, calls=%fused_computation | convolution fusion | flops 2419458048 | bytes 11796484 | tf_op jit(solution)/shard_map/dot_general | solution.py:30
  188.9 3.8 %all-to-all-start.3 = ((bf16[4,4,192,384]{3,2,1,0:T(8,128)(2,1)}), bf16[4,4,192,384]{3,2,1,0:T(8,128)(2,1)S(1)}, u32[]{:S(2)}, u32[]{:S(2)}) async-start(bf16[4,4,192,384]{3,2,1,0:T(8,128)(2,1)} %bitcast.127.refs_10_), calls=%async_computation.3 | async-start | bytes 4718592 | tf_op jit(solution)/shard_map/all_to_all | solution.py:500
  192.8 7.1 %add_convert_fusion.1.refs_11_ = bf16[768,1536]{1,0:T(8,128)(2,1)} fusion(bf16[768,1536]{1,0:T(8,128)(2,1)} %collective-permute-done.11, bf16[1024,768]{1,0:T(8,128)(2,1)} %get-tuple-element.43, bf16[1024,3072]{1,0:T(8,128)(2,1)} %get-tuple-element.44.refs_0_, s32[]{:T(128)S(6)} %select_n.151), kind=kOutput, calls=%fused_computation.1 | convolution fusion | flops 2419458048 | bytes 9437188 | tf_op jit(solution)/shard_map/dot_general | solution.py:30
  199.9 15.3 %up_back.1 = (f32[1024,768]{1,0:T(8,128)}, bf16[1024,768]{1,0:T(8,128)(2,1)}, bf16[1024,768]{1,0:T(8,128)(2,1)}, f32[8,768]{1,0:T(8,128)}) custom-call(bf16[1024,3072]{1,0:T(8,128)(2,1)} %get-tuple-element.44.refs_0_, f32[1024,768]{1,0:T(8,128)} %get-tuple-element.45.refs_1_, f32[1024,768]{1,0:T(8,128)} %get-tuple-element.41.normed_ref.refs_2_, ...), custom_call_target="tpu_custom_call" | custom-call | flops 6039797760 | bytes 28000000 | tf_op jit(solution)/shard_map/up_back/pallas_call | solution.py:335
  227.2 4.5 %all-to-all-start.4 = ((bf16[4,4,48,1920]{3,2,1,0:T(8,128)(2,1)}), bf16[4,4,48,1920]{3,2,1,0:T(8,128)(2,1)S(1)}, u32[]{:S(2)}, u32[]{:S(2)}) async-start(bf16[4,4,48,1920]{3,2,1,0:T(8,128)(2,1)} %tie.19.refs_5_), calls=%async_computation.4 | async-start | bytes 5898240 | tf_op jit(solution)/shard_map/all_to_all | solution.py:500
  235.6 26.1 %attention_back.1 = (bf16[2,512,2304]{2,1,0:T(8,128)(2,1)}, f32[1,2304]{1,0:T(1,128)}) custom-call(s32[12]{0:T(128)} %refs_0_.2, bf16[2,512,2304]{2,1,0:T(8,128)(2,1)} %get-tuple-element.49.refs_1_, bf16[2,12,2,256,256]{4,3,2,1,0:T(8,128)(2,1)} %get-tuple-element.50.refs_2_, bf16[2,512,768]{2,1,0:T(8,128)(2,1)} %bitcast.174, ...), custom_call_target="tpu_custom_call" | custom-call | flops 6442450944 | bytes 20000000 | tf_op jit(solution)/shard_map/attention_back/pallas_call | solution.py:406
  261.7 4.4 %all-to-all-done.4.refs_0_ = bf16[4,4,48,1920]{3,2,1,0:T(8,128)(2,1)S(1)} async-done(((bf16[4,4,48,1920]{3,2,1,0:T(8,128)(2,1)}), bf16[4,4,48,1920]{3,2,1,0:T(8,128)(2,1)S(1)}, u32[]{:S(2)}, u32[]{:S(2)}) %all-to-all-start.4) | async-done | bytes 2949152 | tf_op jit(solution)/shard_map/all_to_all | solution.py:500
  272.7 5.2 %convolution_convert_fusion.2 = bf16[768,1152]{1,0:T(8,128)(2,1)} fusion(bf16[1024,768]{1,0:T(8,128)(2,1)S(1)} %bitcast.145, bf16[1024,2304]{1,0:T(8,128)(2,1)} %tie.23.refs_1_, s32[]{:T(128)S(6)} %select_n.145), kind=kOutput, calls=%fused_computation.5 | convolution fusion | flops 1812824064 | bytes 5701636 | tf_op jit(solution)/shard_map/dot_general | solution.py:30
  286.1 3.6 all-to-all-start.5
  289.7 4.4 %add_convert_fusion.2 = bf16[768,1152]{1,0:T(8,128)(2,1)S(1)} fusion(bf16[768,1152]{1,0:T(8,128)(2,1)} %collective-permute-done.15, bf16[1024,768]{1,0:T(8,128)(2,1)S(1)} %bitcast.146, bf16[1024,2304]{1,0:T(8,128)(2,1)} %tie.23.refs_1_, s32[]{:T(128)S(6)} %select_n.144), kind=kOutput, calls=%fused_computation.3 | convolution fusion | flops 1814593536 | bytes 7471108 | tf_op jit(solution)/shard_map/dot_general | solution.py:30
  299.2 8.6 %tokens_back.1.refs_1_ = bf16[8,2,64,768]{3,2,1,0:T(8,128)(2,1)} custom-call(f32[1024,768]{1,0:T(8,128)} %get-tuple-element.56.refs_0_, bf16[1024,2304]{1,0:T(8,128)(2,1)} %tie.23.refs_1_, bf16[768,2304]{1,0:T(8,128)(2,1)} %get-tuple-element.58.refs_2_, bf16[4,56,1152]{2,1,0:T(8,128)(2,1)} %get-tuple-element.67.refs_3_, ...), custom_call_target="tpu_custom_call" | custom-call | flops 3623878656 | bytes 14000000 | tf_op jit(solution)/shard_map/tokens_back/pallas_call | solution.py:438
  318.8 4.1 %all-to-all-start.6 = ((bf16[8,2,64,768]{3,2,1,0:T(8,128)(2,1)}), bf16[8,2,64,768]{3,2,1,0:T(8,128)(2,1)S(1)}, u32[]{:S(2)}, u32[]{:S(2)}) async-start(bf16[8,2,64,768]{3,2,1,0:T(8,128)(2,1)} %tie.25), calls=%async_computation.6 | async-start | bytes 3145728 | tf_op jit(solution)/shard_map/all_to_all | solution.py:559
  324.0 9.4 %collective-permute-done.19.refs_0_ = bf16[4,56,1152]{2,1,0:T(8,128)(2,1)} collective-permute-done((bf16[4,56,1152]{2,1,0:T(8,128)(2,1)}, bf16[4,56,1152]{2,1,0:T(8,128)(2,1)}, u32[]{:S(2)}, u32[]{:S(2)}) %collective-permute-start.19) | collective-permute-done | bytes 516128 | tf_op jit(solution)/shard_map/ppermute | solution.py:469
  343.4 3.8 %collective-permute-done.21 = bf16[56,1152]{1,0:T(8,128)(2,1)S(1)} collective-permute-done((bf16[56,1152]{1,0:T(8,128)(2,1)S(1)}, bf16[56,1152]{1,0:T(8,128)(2,1)S(1)}, u32[]{:S(2)}, u32[]{:S(2)}) %collective-permute-start.21) | collective-permute-done | bytes 129056 | tf_op jit(solution)/shard_map/ppermute | solution.py:461
  (282 shorter events, 80.2 us)
Async XLA Ops:
  7.3 110.6 %all-gather.3.cloned.1.call-start = ((), (), s32[]{:S(2)}) async-start(), calls=%async_computation.7 | async-start | bytes 10948608 | tf_op jit(solution)/shard_map/all_gather | solution.py:579
  11.2 16.1 %collective-permute-start = (bf16[24,1152]{1,0:T(8,128)(2,1)S(1)}, bf16[24,1152]{1,0:T(8,128)(2,1)S(1)}, u32[]{:S(2)}, u32[]{:S(2)}) collective-permute-start(bf16[24,1152]{1,0:T(8,128)(2,1)S(1)} %get-tuple-element.98), channel_id=1, source_target_pairs={{0,1},{1,0},{2,3},{3,2},{4,5},{5,4},{6,7},{7,6},{8,9},{9,8},{10,11... | collective-permute-start | bytes 165896 | tf_op jit(solution)/shard_map/ppermute | solution.py:456
  12.7 9.7 %all-to-all-start = ((f32[8,1,1282]{2,1,0:T(1,128)}), f32[8,1,1282]{2,1,0:T(1,128)S(1)}, u32[]{:S(2)}, u32[]{:S(2)}) async-start(f32[8,1,1282]{2,1,0:T(1,128)} %all_to_all.36), calls=%async_computation | async-start | bytes 90112 | tf_op jit(solution)/shard_map/all_to_all | solution.py:567
  22.8 57.1 %all-to-all-start.1 = ((bf16[16,64,768]{2,1,0:T(8,128)(2,1)}), bf16[16,64,768]{2,1,0:T(8,128)(2,1)S(1)}, u32[]{:S(2)}, u32[]{:S(2)}) async-start(bf16[16,64,768]{2,1,0:T(8,128)(2,1)} %param.19), calls=%async_computation.1 | async-start | bytes 3145728 | tf_op jit(solution)/shard_map/all_to_all | solution.py:556
  27.3 9.9 %collective-permute-start.3 = (bf16[64,1152]{1,0:T(8,128)(2,1)S(1)}, bf16[64,1152]{1,0:T(8,128)(2,1)S(1)}, u32[]{:S(2)}, u32[]{:S(2)}) collective-permute-start(bf16[64,1152]{1,0:T(8,128)(2,1)S(1)} %fusion.29), channel_id=1, source_target_pairs={{0,24},{8,0},{16,8},{24,16},{1,25},{9,1},{17,9},{25,17},{2,26},{10... | collective-permute-start | bytes 442376 | tf_op jit(solution)/shard_map/ppermute | solution.py:461
  31.0 16.7 %collective-permute-start.2 = (bf16[64,1152]{1,0:T(8,128)(2,1)S(1)}, bf16[64,1152]{1,0:T(8,128)(2,1)S(1)}, u32[]{:S(2)}, u32[]{:S(2)}) collective-permute-start(bf16[64,1152]{1,0:T(8,128)(2,1)S(1)} %fusion.29), channel_id=1, source_target_pairs={{0,16},{8,24},{16,0},{24,8},{1,17},{9,25},{17,1},{25,9},{2,18},{10... | collective-permute-start | bytes 442376 | tf_op jit(solution)/shard_map/ppermute | solution.py:461
  31.0 16.7 %collective-permute-start.1 = (bf16[64,1152]{1,0:T(8,128)(2,1)S(1)}, bf16[64,1152]{1,0:T(8,128)(2,1)S(1)}, u32[]{:S(2)}, u32[]{:S(2)}) collective-permute-start(bf16[64,1152]{1,0:T(8,128)(2,1)S(1)} %fusion.29), channel_id=1, source_target_pairs={{0,8},{8,16},{16,24},{24,0},{1,9},{9,17},{17,25},{25,1},{2,10},{10... | collective-permute-start | bytes 442376 | tf_op jit(solution)/shard_map/ppermute | solution.py:461
  47.8 22.4 %collective-permute-start.6 = (bf16[4,48,1152]{2,1,0:T(8,128)(2,1)S(1)}, bf16[4,48,1152]{2,1,0:T(8,128)(2,1)S(1)}, u32[]{:S(2)}, u32[]{:S(2)}) collective-permute-start(bf16[4,48,1152]{2,1,0:T(8,128)(2,1)S(1)} %pad_maximum_fusion.3.refs_0_), channel_id=1, source_target_pairs={{0,6},{1,7},{2,4},{3,5},{4,2},{5,3},{6,0},{7,1},{8,14},{9,15},{10,... | collective-permute-start | bytes 1327112 | tf_op jit(solution)/shard_map/ppermute | solution.py:469
  49.9 28.7 %collective-permute-start.4 = (bf16[4,48,1152]{2,1,0:T(8,128)(2,1)S(1)}, bf16[4,48,1152]{2,1,0:T(8,128)(2,1)S(1)}, u32[]{:S(2)}, u32[]{:S(2)}) collective-permute-start(bf16[4,48,1152]{2,1,0:T(8,128)(2,1)S(1)} %pad_maximum_fusion.3.refs_0_), channel_id=1, source_target_pairs={{0,2},{1,3},{2,0},{3,1},{4,6},{5,7},{6,4},{7,5},{8,10},{9,11},{10,... | collective-permute-start | bytes 1327112 | tf_op jit(solution)/shard_map/ppermute | solution.py:469
  50.8 27.8 %collective-permute-start.5 = (bf16[4,48,1152]{2,1,0:T(8,128)(2,1)S(1)}, bf16[4,48,1152]{2,1,0:T(8,128)(2,1)}, u32[]{:S(2)}, u32[]{:S(2)}) collective-permute-start(bf16[4,48,1152]{2,1,0:T(8,128)(2,1)S(1)} %pad_maximum_fusion.3.refs_0_), channel_id=1, source_target_pairs={{0,4},{1,5},{2,6},{3,7},{4,0},{5,1},{6,2},{7,3},{8,12},{9,13},{10,... | collective-permute-start | bytes 1327112 | tf_op jit(solution)/shard_map/ppermute | solution.py:469
  51.4 29.8 %collective-permute-start.7 = (bf16[4,48,1152]{2,1,0:T(8,128)(2,1)S(1)}, bf16[4,48,1152]{2,1,0:T(8,128)(2,1)}, u32[]{:S(2)}, u32[]{:S(2)}) collective-permute-start(bf16[4,48,1152]{2,1,0:T(8,128)(2,1)S(1)} %pad_maximum_fusion.3.refs_0_), channel_id=1, source_target_pairs={{0,1},{1,0},{2,3},{3,2},{4,5},{5,4},{6,7},{7,6},{8,9},{9,8},{10,11... | collective-permute-start | bytes 1327112 | tf_op jit(solution)/shard_map/ppermute | solution.py:456
  70.3 10.9 %collective-permute-start.10 = (bf16[4,48,1152]{2,1,0:T(8,128)(2,1)S(1)}, bf16[4,48,1152]{2,1,0:T(8,128)(2,1)}, u32[]{:S(2)}, u32[]{:S(2)}) collective-permute-start(bf16[4,48,1152]{2,1,0:T(8,128)(2,1)S(1)} %collective-permute-done.6.refs_3_), channel_id=1, source_target_pairs={{0,1},{1,0},{2,3},{3,2},{4,5},{5,4},{6,7},{7,6},{8,9},{9,8},{10,11... | collective-permute-start | bytes 1327112 | tf_op jit(solution)/shard_map/ppermute | solution.py:456
  106.5 37.3 %all-to-all-start.2 = ((bf16[16,64,768]{2,1,0:T(8,128)(2,1)}), bf16[16,64,768]{2,1,0:T(8,128)(2,1)S(1)}, u32[]{:S(2)}, u32[]{:S(2)}) async-start(bf16[16,64,768]{2,1,0:T(8,128)(2,1)} %tie.16), calls=%async_computation.2 | async-start | bytes 3145728 | tf_op jit(solution)/shard_map/all_to_all | solution.py:609
  173.8 7.0 %collective-permute-start.12 = (bf16[3072,384]{1,0:T(8,128)(2,1)}, bf16[3072,384]{1,0:T(8,128)(2,1)S(1)}, u32[]{:S(2)}, u32[]{:S(2)}) collective-permute-start(bf16[3072,384]{1,0:T(8,128)(2,1)} %convolution_convert_fusion), channel_id=1, source_target_pairs={{0,1},{1,0},{2,3},{3,2},{4,5},{5,4},{6,7},{7,6},{8,9},{9,8},{10,11... | collective-permute-start | bytes 7077896 | tf_op jit(solution)/shard_map/ppermute | solution.py:456
  180.5 12.2 %collective-permute-start.11 = (bf16[768,1536]{1,0:T(8,128)(2,1)}, bf16[768,1536]{1,0:T(8,128)(2,1)}, u32[]{:S(2)}, u32[]{:S(2)}) collective-permute-start(bf16[768,1536]{1,0:T(8,128)(2,1)} %convolution_convert_fusion.1), channel_id=1, source_target_pairs={{0,1},{1,0},{2,3},{3,2},{4,5},{5,4},{6,7},{7,6},{8,9},{9,8},{10,11... | collective-permute-start | bytes 7077896 | tf_op jit(solution)/shard_map/ppermute | solution.py:456
  188.9 33.8 %all-to-all-start.3 = ((bf16[4,4,192,384]{3,2,1,0:T(8,128)(2,1)}), bf16[4,4,192,384]{3,2,1,0:T(8,128)(2,1)S(1)}, u32[]{:S(2)}, u32[]{:S(2)}) async-start(bf16[4,4,192,384]{3,2,1,0:T(8,128)(2,1)} %bitcast.127.refs_10_), calls=%async_computation.3 | async-start | bytes 4718592 | tf_op jit(solution)/shard_map/all_to_all | solution.py:500
  227.2 38.9 %all-to-all-start.4 = ((bf16[4,4,48,1920]{3,2,1,0:T(8,128)(2,1)}), bf16[4,4,48,1920]{3,2,1,0:T(8,128)(2,1)S(1)}, u32[]{:S(2)}, u32[]{:S(2)}) async-start(bf16[4,4,48,1920]{3,2,1,0:T(8,128)(2,1)} %tie.19.refs_5_), calls=%async_computation.4 | async-start | bytes 5898240 | tf_op jit(solution)/shard_map/all_to_all | solution.py:500
  277.9 11.8 %collective-permute-start.15 = (bf16[768,1152]{1,0:T(8,128)(2,1)}, bf16[768,1152]{1,0:T(8,128)(2,1)}, u32[]{:S(2)}, u32[]{:S(2)}) collective-permute-start(bf16[768,1152]{1,0:T(8,128)(2,1)} %convolution_convert_fusion.2), channel_id=1, source_target_pairs={{0,1},{1,0},{2,3},{3,2},{4,5},{5,4},{6,7},{7,6},{8,9},{9,8},{10,11... | collective-permute-start | bytes 5308424 | tf_op jit(solution)/shard_map/ppermute | solution.py:456
  281.3 26.4 %collective-permute-start.24 = (bf16[48,3456]{1,0:T(8,128)(2,1)}, bf16[48,3456]{1,0:T(8,128)(2,1)}, u32[]{:S(2)}, u32[]{:S(2)}) collective-permute-start(bf16[48,3456]{1,0:T(8,128)(2,1)} %get-tuple-element.70.refs_2_), channel_id=1, source_target_pairs={{0,8},{8,16},{16,24},{24,0},{1,9},{9,17},{17,25},{25,1},{2,10},{10... | collective-permute-start | bytes 995336 | tf_op jit(solution)/shard_map/ppermute | solution.py:461
  282.7 25.2 %collective-permute-start.25 = (bf16[48,3456]{1,0:T(8,128)(2,1)}, bf16[48,3456]{1,0:T(8,128)(2,1)}, u32[]{:S(2)}, u32[]{:S(2)}) collective-permute-start(bf16[48,3456]{1,0:T(8,128)(2,1)} %get-tuple-element.71.refs_3_), channel_id=1, source_target_pairs={{0,16},{8,24},{16,0},{24,8},{1,17},{9,25},{17,1},{25,9},{2,18},{10... | collective-permute-start | bytes 995336 | tf_op jit(solution)/shard_map/ppermute | solution.py:461
  283.7 24.2 %collective-permute-start.26 = (bf16[48,3456]{1,0:T(8,128)(2,1)S(1)}, bf16[48,3456]{1,0:T(8,128)(2,1)}, u32[]{:S(2)}, u32[]{:S(2)}) collective-permute-start(bf16[48,3456]{1,0:T(8,128)(2,1)S(1)} %copy-done.14), channel_id=1, source_target_pairs={{0,24},{8,0},{16,8},{24,16},{1,25},{9,1},{17,9},{25,17},{2,26},{10... | collective-permute-start | bytes 995336 | tf_op jit(solution)/shard_map/ppermute | solution.py:461
  286.1 31.5 %all-to-all-start.5 = ((bf16[8,2,64,768]{3,2,1,0:T(8,128)(2,1)}), bf16[8,2,64,768]{3,2,1,0:T(8,128)(2,1)S(1)}, u32[]{:S(2)}, u32[]{:S(2)}) async-start(bf16[8,2,64,768]{3,2,1,0:T(8,128)(2,1)} %tie.21), calls=%async_computation.5 | async-start | bytes 3145728 | tf_op jit(solution)/shard_map/all_to_all | solution.py:559
  295.8 28.2 %collective-permute-start.17 = (bf16[4,56,1152]{2,1,0:T(8,128)(2,1)}, bf16[4,56,1152]{2,1,0:T(8,128)(2,1)}, u32[]{:S(2)}, u32[]{:S(2)}) collective-permute-start(bf16[4,56,1152]{2,1,0:T(8,128)(2,1)} %get-tuple-element.66.refs_4_), channel_id=1, source_target_pairs={{0,2},{1,3},{2,0},{3,1},{4,6},{5,7},{6,4},{7,5},{8,10},{9,11},{10,... | collective-permute-start | bytes 1548296 | tf_op jit(solution)/shard_map/ppermute | solution.py:469
  297.7 26.3 %collective-permute-start.18 = (bf16[4,56,1152]{2,1,0:T(8,128)(2,1)}, bf16[4,56,1152]{2,1,0:T(8,128)(2,1)}, u32[]{:S(2)}, u32[]{:S(2)}) collective-permute-start(bf16[4,56,1152]{2,1,0:T(8,128)(2,1)} %get-tuple-element.65.refs_5_), channel_id=1, source_target_pairs={{0,4},{1,5},{2,6},{3,7},{4,0},{5,1},{6,2},{7,3},{8,12},{9,13},{10,... | collective-permute-start | bytes 1548296 | tf_op jit(solution)/shard_map/ppermute | solution.py:469
  307.7 25.7 %collective-permute-start.19 = (bf16[4,56,1152]{2,1,0:T(8,128)(2,1)}, bf16[4,56,1152]{2,1,0:T(8,128)(2,1)}, u32[]{:S(2)}, u32[]{:S(2)}) collective-permute-start(bf16[4,56,1152]{2,1,0:T(8,128)(2,1)} %get-tuple-element.64.refs_6_), channel_id=1, source_target_pairs={{0,6},{1,7},{2,4},{3,5},{4,2},{5,3},{6,0},{7,1},{8,14},{9,15},{10,... | collective-permute-start | bytes 1548296 | tf_op jit(solution)/shard_map/ppermute | solution.py:469
  313.7 26.3 %collective-permute-start.29 = (f32[96,384]{1,0:T(8,128)}, f32[96,384]{1,0:T(8,128)}, u32[]{:S(2)}, u32[]{:S(2)}) collective-permute-start(f32[96,384]{1,0:T(8,128)} %get-tuple-element.82), channel_id=1, source_target_pairs={{0,1},{1,0},{2,3},{3,2},{4,5},{5,4},{6,7},{7,6},{8,9},{9,8},{10,11... | collective-permute-start | bytes 442376 | tf_op jit(solution)/shard_map/ppermute | solution.py:456
  314.3 8.6 %collective-permute-start.27 = (f32[24,384]{1,0:T(8,128)}, f32[24,384]{1,0:T(8,128)S(1)}, u32[]{:S(2)}, u32[]{:S(2)}) collective-permute-start(f32[24,384]{1,0:T(8,128)} %get-tuple-element.100), channel_id=1, source_target_pairs={{0,1},{1,0},{2,3},{3,2},{4,5},{5,4},{6,7},{7,6},{8,9},{9,8},{10,11... | collective-permute-start | bytes 110600 | tf_op jit(solution)/shard_map/ppermute | solution.py:456
  318.8 31.1 %all-to-all-start.6 = ((bf16[8,2,64,768]{3,2,1,0:T(8,128)(2,1)}), bf16[8,2,64,768]{3,2,1,0:T(8,128)(2,1)S(1)}, u32[]{:S(2)}, u32[]{:S(2)}) async-start(bf16[8,2,64,768]{3,2,1,0:T(8,128)(2,1)} %tie.25), calls=%async_computation.6 | async-start | bytes 3145728 | tf_op jit(solution)/shard_map/all_to_all | solution.py:559
  322.9 16.4 %collective-permute-start.28 = (f32[24,1536]{1,0:T(8,128)}, f32[24,1536]{1,0:T(8,128)S(1)}, u32[]{:S(2)}, u32[]{:S(2)}) collective-permute-start(f32[24,1536]{1,0:T(8,128)} %get-tuple-element.84), channel_id=1, source_target_pairs={{0,1},{1,0},{2,3},{3,2},{4,5},{5,4},{6,7},{7,6},{8,9},{9,8},{10,11... | collective-permute-start | bytes 442376 | tf_op jit(solution)/shard_map/ppermute | solution.py:456
  335.1 8.3 %collective-permute-start.20 = (bf16[56,1152]{1,0:T(8,128)(2,1)S(1)}, bf16[56,1152]{1,0:T(8,128)(2,1)S(1)}, u32[]{:S(2)}, u32[]{:S(2)}) collective-permute-start(bf16[56,1152]{1,0:T(8,128)(2,1)S(1)} %get-tuple-element.78), channel_id=1, source_target_pairs={{0,8},{8,16},{16,24},{24,0},{1,9},{9,17},{17,25},{25,1},{2,10},{10... | collective-permute-start | bytes 387080 | tf_op jit(solution)/shard_map/ppermute | solution.py:461
  335.2 12.0 %collective-permute-start.21 = (bf16[56,1152]{1,0:T(8,128)(2,1)S(1)}, bf16[56,1152]{1,0:T(8,128)(2,1)S(1)}, u32[]{:S(2)}, u32[]{:S(2)}) collective-permute-start(bf16[56,1152]{1,0:T(8,128)(2,1)S(1)} %get-tuple-element.80), channel_id=1, source_target_pairs={{0,16},{8,24},{16,0},{24,8},{1,17},{9,25},{17,1},{25,9},{2,18},{10... | collective-permute-start | bytes 387080 | tf_op jit(solution)/shard_map/ppermute | solution.py:461
  336.5 10.7 %collective-permute-start.22 = (bf16[56,1152]{1,0:T(8,128)(2,1)S(1)}, bf16[56,1152]{1,0:T(8,128)(2,1)S(1)}, u32[]{:S(2)}, u32[]{:S(2)}) collective-permute-start(bf16[56,1152]{1,0:T(8,128)(2,1)S(1)} %get-tuple-element.79), channel_id=1, source_target_pairs={{0,24},{8,0},{16,8},{24,16},{1,25},{9,1},{17,9},{25,17},{2,26},{10... | collective-permute-start | bytes 387080 | tf_op jit(solution)/shard_map/ppermute | solution.py:461
  (50 other events, 296.4 us)
Sparse Core Ops, SparseCore 0:
  11.3 106.6 all-gather.2
where the time goes:
time: 365 us; the launch traced here: 359 us
  Pallas kernels  113 us (31%)
  waiting for transfers between devices  77.2 us (21%)
  starting transfers between devices  52.8 us (14%)
  local copies, waits for them, and re-layouts  44.1 us (12%)
  matrix products  39 us (11%)
  other arithmetic  17.5 us (5%)
  between operations  15.3 us (4%)
    dot_general x8, matrix products, dot_tn(): lax.dot_general(a, b, (((0,), (0,)), ((), ())), preferred_element_type=F32)  39 us
    ppermute x6, waiting for transfers between devices, hop(): lax.ppermute(a, 'fsdp', [(i, i ^ 2 * away) for i in range(lax.axis_size('...  36.5 us
    pallas_call x1, Pallas kernels, attention_back(): pl.pallas_call(without(attention_back_kernel, 4, len(earlier)), grid_spec...  26.1 us
    pallas_call x1, Pallas kernels, qkv_attention(): pl.pallas_call(functools.partial(attention_kernel, pieces if isinstance(p...  25.2 us
    pallas_call x1, Pallas kernels, down_and_back(): pl.pallas_call(down_kernel, grid=(rows // tile,), in_specs=[rows_of(tile,...  22.6 us
    ppermute x9, waiting for transfers between devices, z_shift(): return lax.ppermute(a, 'dp', [(i, (i + k) % n) for i in range(n)])  21.2 us
    unnamed x97, local copies, waits for them, and re-layouts  15.7 us
    pallas_call x1, Pallas kernels, out_up(): pl.pallas_call(functools.partial(up_kernel, chunk), grid=(rows // tile,),...  15.7 us
  transfers between devices with their start and end apart: 38, of which 15 were waited for; matrix products, arithmetic and copies ran while one was open for 19% of the time, Pallas kernels for 25%

commit v1 on v0

--- a/solution.py
+++ b/solution.py
@@ -237,6 +237,20 @@
     )(mixed, x, vecs, up_b, out_w, *up_w)
 
 
+def chunks(w_ref):
+    width = w_ref.shape[2]
+    each = width // w_ref.shape[1]
+    for i in range(w_ref.shape[0] // each):
+        yield slice(i * width, (i + 1) * width), w_ref[i * each : (i + 1) * each].reshape(width, width)
+
+
+def down_of(act_ref, w_ref):
+    value = 0.0
+    for cols, weight in chunks(w_ref):
+        value = value + dot(act_ref[:, cols], weight)
+    return value
+
+
 def down_kernel(act_ref, slope_ref, normed_ref, g_ref, vec_ref, w_ref, *refs):
     out_ref, two_ref, down_low_ref, up_low_ref, sums_ref, up_sum_ref = refs
     width = normed_ref.shape[1]
@@ -247,7 +261,7 @@
         up_sum_ref[...] = jnp.zeros_like(up_sum_ref)
 
     hidden = normed_ref[...] * vec_ref[0:1] + vec_ref[1:2]
-    normed, scale = norm(hidden + dot(act_ref[...], w_ref[...]) + vec_ref[2:3])
+    normed, scale = norm(hidden + down_of(act_ref, w_ref) + vec_ref[2:3])
     out_ref[...] = (normed * vec_ref[3:4] + vec_ref[4:5]).astype(BF).reshape(out_ref.shape)
     g = g_ref[...].reshape(normed_ref.shape).astype(F32)
     two = norm_back(normed, scale, g * vec_ref[3:4])
@@ -257,9 +271,8 @@
     sums_ref[0:1] += jnp.sum(g * normed, axis=0, keepdims=True)
     sums_ref[1:2] += jnp.sum(g, axis=0, keepdims=True)
     sums_ref[2:3] += jnp.sum(low.astype(F32), axis=0, keepdims=True)
-    for start in range(0, w_ref.shape[0], width):
-        cols = slice(start, start + width)
-        up_low = (dot_nt(low, w_ref[cols, :]) * slope_ref[:, cols].astype(F32)).astype(BF)
+    for cols, weight in chunks(w_ref):
+        up_low = (dot_nt(low, weight) * slope_ref[:, cols].astype(F32)).astype(BF)
         up_low_ref[:, cols] = up_low
         up_sum_ref[:, cols] += jnp.sum(up_low.astype(F32), axis=0, keepdims=True)
 
@@ -282,7 +295,7 @@
             rows_of(tile, width),
             given(tile, piece, length, width),
             whole(vecs.shape),
-            whole(down_w.shape),
+            whole((down_w.shape[0], wide // down_w.shape[0], width)),
         ],
         out_specs=[
             given(tile, piece, length, width),
@@ -575,11 +588,12 @@
     every = notes[:, per * piece : per * piece + n_vec].astype(BF)
     x3 = deal(after(tokens, notes))
     folds = up_s.shape[1] // width
-    own = jnp.concatenate([out_s] + [up_s[:, j * width : (j + 1) * width] for j in range(folds)] + [down_s], 0)
-    ffn_w = lax.all_gather(own[None], BOTH, axis=0, tiled=True)
-    n = out_s.shape[0]
-    out_w, *up_w = (ffn_w[:, j * n : (j + 1) * n].reshape(width, width) for j in range(1 + folds))
-    down_w = ffn_w[:, (1 + folds) * n :].reshape(-1, width)
+    own = jnp.concatenate([down_s, out_s] + [up_s[:, j * width : (j + 1) * width] for j in range(folds)], 0)
+    down_w = ffn_w = lax.all_gather(own[None], BOTH, axis=0, tiled=True)
+    n, m = out_s.shape[0], down_s.shape[0]
+    out_w, *up_w = (ffn_w[:, m + j * n : m + (j + 1) * n].reshape(width, width) for j in range(1 + folds))
+    if not fast:
+        down_w = ffn_w[:, :m].reshape(-1, width, width)
     if fast:
         chip = core_order(core, half_of(qkv_s, core), core_swap(half_of(qkv_s, 1 - core)), 0)
         every = jnp.pad(every, ((0, 8), (0, chip.shape[1] - n_vec)))

time: 365 us -> 360 us (0.986)
  local copies, waits for them, and re-layouts: 44.1 us -> 38.9 us
    slice x2 -> x1, local copies, waits for them, and re-layouts: 10.1 us -> 5.27 us  [local(): ffn_w[:, m + j * n:m + (j + 1) * n].reshape(width, width)]
  transfers between devices with their start and end apart: 38 -> 38, of which waited for: 15 -> 15; matrix products, arithmetic and copies ran while one was open for 19% -> 18% of each run, Pallas kernels for 25% -> 26%
where the time goes in v1:
time: 360 us; the launch traced here: 354 us
  Pallas kernels  113 us (31%)
  waiting for transfers between devices  77.2 us (21%)
  starting transfers between devices  52.9 us (15%)
  local copies, waits for them, and re-layouts  38.9 us (11%)
  matrix products  38.9 us (11%)
  other arithmetic  17.5 us (5%)
  between operations  15.3 us (4%)
    dot_general x8, matrix products, dot_tn(): lax.dot_general(a, b, (((0,), (0,)), ((), ())), preferred_element_type=F32)  38.9 us
    ppermute x6, waiting for transfers between devices, hop(): lax.ppermute(a, 'fsdp', [(i, i ^ 2 * away) for i in range(lax.axis_size('...  36.5 us
    pallas_call x1, Pallas kernels, attention_back(): pl.pallas_call(without(attention_back_kernel, 4, len(earlier)), grid_spec...  26.1 us
    pallas_call x1, Pallas kernels, qkv_attention(): pl.pallas_call(functools.partial(attention_kernel, pieces if isinstance(p...  25.1 us
    pallas_call x1, Pallas kernels, down_and_back(): pl.pallas_call(down_kernel, grid=(rows // tile,), in_specs=[rows_of(tile,...  22.7 us
    ppermute x9, waiting for transfers between devices, z_shift(): return lax.ppermute(a, 'dp', [(i, (i + k) % n) for i in range(n)])  21.2 us
    pallas_call x1, Pallas kernels, out_up(): pl.pallas_call(functools.partial(up_kernel, chunk), grid=(rows // tile,),...  15.7 us
    unnamed x97, local copies, waits for them, and re-layouts  15.6 us
  transfers between devices with their start and end apart: 38, of which 15 were waited for; matrix products, arithmetic and copies ran while one was open for 18% of the time, Pallas kernels for 26%

profile of v1, /device:TPU:0, one launch (start us, length us, event | category | flops | bytes accessed | tf_op | source)
XLA Modules:
  0.0 354.1 jit_solution(9043492798378341014)
XLA Ops:
  7.4 2.8 copy.128.refs_0_
  12.6 4.8 %all-to-all-start = ((f32[8,1,1282]{2,1,0:T(1,128)}), f32[8,1,1282]{2,1,0:T(1,128)S(1)}, u32[]{:S(2)}, u32[]{:S(2)}) async-start(f32[8,1,1282]{2,1,0:T(1,128)} %all_to_all.36), calls=%async_computation | async-start | bytes 90112 | tf_op jit(solution)/shard_map/all_to_all | solution.py:580
  18.1 4.3 %all-to-all-done = f32[8,1,1282]{2,1,0:T(1,128)S(1)} async-done(((f32[8,1,1282]{2,1,0:T(1,128)}), f32[8,1,1282]{2,1,0:T(1,128)S(1)}, u32[]{:S(2)}, u32[]{:S(2)}) %all-to-all-start) | async-done | bytes 41056 | tf_op jit(solution)/shard_map/all_to_all | solution.py:580
  22.7 3.6 %all-to-all-start.1 = ((bf16[16,64,768]{2,1,0:T(8,128)(2,1)}), bf16[16,64,768]{2,1,0:T(8,128)(2,1)S(1)}, u32[]{:S(2)}, u32[]{:S(2)}) async-start(bf16[16,64,768]{2,1,0:T(8,128)(2,1)} %param.19), calls=%async_computation.1 | async-start | bytes 3145728 | tf_op jit(solution)/shard_map/all_to_all | solution.py:569
  27.2 3.7 %collective-permute-start.3 = (bf16[64,1152]{1,0:T(8,128)(2,1)S(1)}, bf16[64,1152]{1,0:T(8,128)(2,1)S(1)}, u32[]{:S(2)}, u32[]{:S(2)}) collective-permute-start(bf16[64,1152]{1,0:T(8,128)(2,1)S(1)} %fusion.29), channel_id=1, source_target_pairs={{0,24},{8,0},{16,8},{24,16},{1,25},{9,1},{17,9},{25,17},{2,26},{10... | collective-permute-start | bytes 442376 | tf_op jit(solution)/shard_map/ppermute | solution.py:474
  31.9 5.2 %collective-permute-done.3 = bf16[64,1152]{1,0:T(8,128)(2,1)S(1)} collective-permute-done((bf16[64,1152]{1,0:T(8,128)(2,1)S(1)}, bf16[64,1152]{1,0:T(8,128)(2,1)S(1)}, u32[]{:S(2)}, u32[]{:S(2)}) %collective-permute-start.3) | collective-permute-done | bytes 147488 | tf_op jit(solution)/shard_map/ppermute | solution.py:474
  37.2 10.5 %collective-permute-done.2 = bf16[64,1152]{1,0:T(8,128)(2,1)S(1)} collective-permute-done((bf16[64,1152]{1,0:T(8,128)(2,1)S(1)}, bf16[64,1152]{1,0:T(8,128)(2,1)S(1)}, u32[]{:S(2)}, u32[]{:S(2)}) %collective-permute-start.2) | collective-permute-done | bytes 147488 | tf_op jit(solution)/shard_map/ppermute | solution.py:474
  51.4 18.7 %collective-permute-done.6.refs_3_ = bf16[4,48,1152]{2,1,0:T(8,128)(2,1)S(1)} collective-permute-done((bf16[4,48,1152]{2,1,0:T(8,128)(2,1)S(1)}, bf16[4,48,1152]{2,1,0:T(8,128)(2,1)S(1)}, u32[]{:S(2)}, u32[]{:S(2)}) %collective-permute-start.6) | collective-permute-done | bytes 442400 | tf_op jit(solution)/shard_map/ppermute | solution.py:482
  70.2 8.3 %collective-permute-done.4.refs_1_ = bf16[4,48,1152]{2,1,0:T(8,128)(2,1)S(1)} collective-permute-done((bf16[4,48,1152]{2,1,0:T(8,128)(2,1)S(1)}, bf16[4,48,1152]{2,1,0:T(8,128)(2,1)S(1)}, u32[]{:S(2)}, u32[]{:S(2)}) %collective-permute-start.4) | collective-permute-done | bytes 442400 | tf_op jit(solution)/shard_map/ppermute | solution.py:482
  81.3 25.1 %qkv_attention.1 = (bf16[2,512,2304]{2,1,0:T(8,128)(2,1)}, bf16[2,512,768]{2,1,0:T(8,128)(2,1)}, bf16[2,12,2,256,256]{4,3,2,1,0:T(8,128)(2,1)}, bf16[768,2304]{1,0:T(8,128)(2,1)}) custom-call(s32[3]{0:T(128)} %pad_add_fusion.place_ref, s32[12]{0:T(128)} %refs_0_.2, bf16[2,512,768]{2,1,0:T(8,128)(2,1)} %bitcast.140, f32[1,2304]{1,0:T(1,128)} %fusion.41.b_ref, ...), custom_call_target="tpu_custom_call" | custom-call | flops 6845104128 | bytes 22000000 | tf_op jit(solution)/shard_map/qkv_attention/pallas_call | solution.py:144
  106.4 4.1 %all-to-all-start.2 = ((bf16[16,64,768]{2,1,0:T(8,128)(2,1)}), bf16[16,64,768]{2,1,0:T(8,128)(2,1)S(1)}, u32[]{:S(2)}, u32[]{:S(2)}) async-start(bf16[16,64,768]{2,1,0:T(8,128)(2,1)} %tie.16), calls=%async_computation.2 | async-start | bytes 3145728 | tf_op jit(solution)/shard_map/all_to_all | solution.py:623
  113.0 4.9 %all-gather.3.cloned.1.call-done = bf16[6912,768]{1,0:T(8,128)(2,1)} async-done(((bf16[216,768]{1,0:T(8,128)(2,1)}), bf16[6912,768]{1,0:T(8,128)(2,1)}) %all-gather.3.cloned.1.call-update) | async-done | bytes 10616848 | tf_op jit(solution)/shard_map/all_gather | solution.py:592
  117.9 5.3 %fusion.45 = (bf16[32,24,768]{2,1,0:T(8,128)(2,1)}, bf16[32,24,768]{2,1,0:T(8,128)(2,1)}, bf16[32,24,768]{2,1,0:T(8,128)(2,1)}, bf16[32,24,768]{2,1,0:T(8,128)(2,1)}, bf16[32,24,768]{2,1,0:T(8,128)(2,1)}) fusion(bf16[32,216,768]{2,1,0:T(8,128)(2,1)} %bitcast.154), kind=kLoop, calls=%fused_computation.141 | loop fusion | bytes 11796480 | tf_op jit(solution)/shard_map/slice | solution.py:594
  123.2 15.7 %out_up.1 = (f32[1024,768]{1,0:T(8,128)}, f32[1024,1]{1,0:T(8,128)}, bf16[1024,768]{1,0:T(8,128)(2,1)}, bf16[1024,3072]{1,0:T(8,128)(2,1)}, bf16[1024,3072]{1,0:T(8,128)(2,1)}) custom-call(bf16[1024,768]{1,0:T(8,128)(2,1)} %bitcast.158, bf16[1024,768]{1,0:T(8,128)(2,1)} %bitcast.141, f32[3,768]{1,0:T(4,128)} %pad_maximum_fusion.7.vec_ref, ...), custom_call_target="tpu_custom_call" | custom-call | flops 6039797760 | bytes 38000000 | tf_op jit(solution)/shard_map/out_up/pallas_call | solution.py:212
  140.0 22.7 %down_and_back.1 = (bf16[8,2,64,768]{3,2,1,0:T(8,128)(2,1)}, f32[1024,768]{1,0:T(8,128)}, bf16[1024,768]{1,0:T(8,128)(2,1)}, bf16[1024,3072]{1,0:T(8,128)(2,1)}, f32[8,768]{1,0:T(8,128)}, /*index=5*/f32[1,3072]{1,0:T(1,128)}) custom-call(bf16[1024,3072]{1,0:T(8,128)(2,1)} %get-tuple-element.39.refs_1_.act_ref, ...), custom_call_target="tpu_custom_call" | custom-call | flops 9663676416 | bytes 38000000 | tf_op jit(solution)/shard_map/down_and_back/pallas_call | solution.py:289
  162.7 6.1 %convolution_convert_fusion = bf16[3072,384]{1,0:T(8,128)(2,1)} fusion(bf16[1024,3072]{1,0:T(8,128)(2,1)S(1)} %bitcast.136, bf16[1024,768]{1,0:T(8,128)(2,1)} %get-tuple-element.47, s32[]{:T(128)S(6)} %select_n.154), kind=kOutput, calls=%fused_computation.2 | convolution fusion | flops 2417098752 | bytes 9437188 | tf_op jit(solution)/shard_map/dot_general | solution.py:30
  169.2 6.4 %convolution_convert_fusion.1 = bf16[768,1536]{1,0:T(8,128)(2,1)} fusion(bf16[1024,768]{1,0:T(8,128)(2,1)} %get-tuple-element.43, bf16[1024,3072]{1,0:T(8,128)(2,1)} %get-tuple-element.44.refs_0_, s32[]{:T(128)S(6)} %select_n.152), kind=kOutput, calls=%fused_computation.4 | convolution fusion | flops 2417098752 | bytes 7077892 | tf_op jit(solution)/shard_map/dot_general | solution.py:30
  175.8 6.4 %add_convert_fusion = bf16[3072,384]{1,0:T(8,128)(2,1)S(1)} fusion(bf16[3072,384]{1,0:T(8,128)(2,1)S(1)} %collective-permute-done.12, bf16[1024,3072]{1,0:T(8,128)(2,1)} %get-tuple-element.39.refs_1_.act_ref, bf16[1024,768]{1,0:T(8,128)(2,1)} %get-tuple-element.47, s32[]{:T(128)S(6)} %select_n.153), kind=kOutput, calls=%fused_computation | convolution fusion | flops 2419458048 | bytes 11796484 | tf_op jit(solution)/shard_map/dot_general | solution.py:30
  183.9 3.8 %all-to-all-start.3 = ((bf16[4,4,192,384]{3,2,1,0:T(8,128)(2,1)}), bf16[4,4,192,384]{3,2,1,0:T(8,128)(2,1)S(1)}, u32[]{:S(2)}, u32[]{:S(2)}) async-start(bf16[4,4,192,384]{3,2,1,0:T(8,128)(2,1)} %bitcast.126.refs_10_), calls=%async_computation.3 | async-start | bytes 4718592 | tf_op jit(solution)/shard_map/all_to_all | solution.py:513
  187.8 7.1 %add_convert_fusion.1.refs_11_ = bf16[768,1536]{1,0:T(8,128)(2,1)} fusion(bf16[768,1536]{1,0:T(8,128)(2,1)} %collective-permute-done.11, bf16[1024,768]{1,0:T(8,128)(2,1)} %get-tuple-element.43, bf16[1024,3072]{1,0:T(8,128)(2,1)} %get-tuple-element.44.refs_0_, s32[]{:T(128)S(6)} %select_n.151), kind=kOutput, calls=%fused_computation.1 | convolution fusion | flops 2419458048 | bytes 9437188 | tf_op jit(solution)/shard_map/dot_general | solution.py:30
  194.9 15.3 %up_back.1 = (f32[1024,768]{1,0:T(8,128)}, bf16[1024,768]{1,0:T(8,128)(2,1)}, bf16[1024,768]{1,0:T(8,128)(2,1)}, f32[8,768]{1,0:T(8,128)}) custom-call(bf16[1024,3072]{1,0:T(8,128)(2,1)} %get-tuple-element.44.refs_0_, f32[1024,768]{1,0:T(8,128)} %get-tuple-element.45.refs_1_, f32[1024,768]{1,0:T(8,128)} %get-tuple-element.41.normed_ref.refs_2_, ...), custom_call_target="tpu_custom_call" | custom-call | flops 6039797760 | bytes 28000000 | tf_op jit(solution)/shard_map/up_back/pallas_call | solution.py:348
  222.1 4.5 %all-to-all-start.4 = ((bf16[4,4,48,1920]{3,2,1,0:T(8,128)(2,1)}), bf16[4,4,48,1920]{3,2,1,0:T(8,128)(2,1)S(1)}, u32[]{:S(2)}, u32[]{:S(2)}) async-start(bf16[4,4,48,1920]{3,2,1,0:T(8,128)(2,1)} %tie.19.refs_5_), calls=%async_computation.4 | async-start | bytes 5898240 | tf_op jit(solution)/shard_map/all_to_all | solution.py:513
  230.5 26.1 %attention_back.1 = (bf16[2,512,2304]{2,1,0:T(8,128)(2,1)}, f32[1,2304]{1,0:T(1,128)}) custom-call(s32[12]{0:T(128)} %refs_0_.2, bf16[2,512,2304]{2,1,0:T(8,128)(2,1)} %get-tuple-element.49.refs_1_, bf16[2,12,2,256,256]{4,3,2,1,0:T(8,128)(2,1)} %get-tuple-element.50.refs_2_, bf16[2,512,768]{2,1,0:T(8,128)(2,1)} %bitcast.172, ...), custom_call_target="tpu_custom_call" | custom-call | flops 6442450944 | bytes 20000000 | tf_op jit(solution)/shard_map/attention_back/pallas_call | solution.py:419
  256.6 4.4 %all-to-all-done.4.refs_0_ = bf16[4,4,48,1920]{3,2,1,0:T(8,128)(2,1)S(1)} async-done(((bf16[4,4,48,1920]{3,2,1,0:T(8,128)(2,1)}), bf16[4,4,48,1920]{3,2,1,0:T(8,128)(2,1)S(1)}, u32[]{:S(2)}, u32[]{:S(2)}) %all-to-all-start.4) | async-done | bytes 2949152 | tf_op jit(solution)/shard_map/all_to_all | solution.py:513
  267.6 5.2 %convolution_convert_fusion.2 = bf16[768,1152]{1,0:T(8,128)(2,1)} fusion(bf16[1024,768]{1,0:T(8,128)(2,1)S(1)} %bitcast.142, bf16[1024,2304]{1,0:T(8,128)(2,1)} %tie.23.refs_1_, s32[]{:T(128)S(6)} %select_n.145), kind=kOutput, calls=%fused_computation.5 | convolution fusion | flops 1812824064 | bytes 5701636 | tf_op jit(solution)/shard_map/dot_general | solution.py:30
  273.3 2.8 collective-permute-done.16
  280.9 3.6 %all-to-all-start.5 = ((bf16[8,2,64,768]{3,2,1,0:T(8,128)(2,1)}), bf16[8,2,64,768]{3,2,1,0:T(8,128)(2,1)S(1)}, u32[]{:S(2)}, u32[]{:S(2)}) async-start(bf16[8,2,64,768]{3,2,1,0:T(8,128)(2,1)} %tie.21), calls=%async_computation.5 | async-start | bytes 3145728 | tf_op jit(solution)/shard_map/all_to_all | solution.py:572
  284.5 4.4 %add_convert_fusion.2 = bf16[768,1152]{1,0:T(8,128)(2,1)S(1)} fusion(bf16[768,1152]{1,0:T(8,128)(2,1)} %collective-permute-done.15, bf16[1024,768]{1,0:T(8,128)(2,1)S(1)} %bitcast.143, bf16[1024,2304]{1,0:T(8,128)(2,1)} %tie.23.refs_1_, s32[]{:T(128)S(6)} %select_n.144), kind=kOutput, calls=%fused_computation.3 | convolution fusion | flops 1814593536 | bytes 7471108 | tf_op jit(solution)/shard_map/dot_general | solution.py:30
  294.0 8.5 %tokens_back.1.refs_1_ = bf16[8,2,64,768]{3,2,1,0:T(8,128)(2,1)} custom-call(f32[1024,768]{1,0:T(8,128)} %get-tuple-element.56.refs_0_, bf16[1024,2304]{1,0:T(8,128)(2,1)} %tie.23.refs_1_, bf16[768,2304]{1,0:T(8,128)(2,1)} %get-tuple-element.58.refs_2_, bf16[4,56,1152]{2,1,0:T(8,128)(2,1)} %get-tuple-element.67.refs_3_, ...), custom_call_target="tpu_custom_call" | custom-call | flops 3623878656 | bytes 14000000 | tf_op jit(solution)/shard_map/tokens_back/pallas_call | solution.py:451
  313.6 4.1 %all-to-all-start.6 = ((bf16[8,2,64,768]{3,2,1,0:T(8,128)(2,1)}), bf16[8,2,64,768]{3,2,1,0:T(8,128)(2,1)S(1)}, u32[]{:S(2)}, u32[]{:S(2)}) async-start(bf16[8,2,64,768]{3,2,1,0:T(8,128)(2,1)} %tie.25), calls=%async_computation.6 | async-start | bytes 3145728 | tf_op jit(solution)/shard_map/all_to_all | solution.py:572
  318.9 9.4 %collective-permute-done.19.refs_0_ = bf16[4,56,1152]{2,1,0:T(8,128)(2,1)} collective-permute-done((bf16[4,56,1152]{2,1,0:T(8,128)(2,1)}, bf16[4,56,1152]{2,1,0:T(8,128)(2,1)}, u32[]{:S(2)}, u32[]{:S(2)}) %collective-permute-start.19) | collective-permute-done | bytes 516128 | tf_op jit(solution)/shard_map/ppermute | solution.py:482
  338.2 3.8 %collective-permute-done.21 = bf16[56,1152]{1,0:T(8,128)(2,1)S(1)} collective-permute-done((bf16[56,1152]{1,0:T(8,128)(2,1)S(1)}, bf16[56,1152]{1,0:T(8,128)(2,1)S(1)}, u32[]{:S(2)}, u32[]{:S(2)}) %collective-permute-start.21) | collective-permute-done | bytes 129056 | tf_op jit(solution)/shard_map/ppermute | solution.py:474
  (281 shorter events, 77.2 us)
Async XLA Ops:
  7.3 110.6 %all-gather.3.cloned.1.call-start = ((), (), s32[]{:S(2)}) async-start(), calls=%async_computation.7 | async-start | bytes 10948608 | tf_op jit(solution)/shard_map/all_gather | solution.py:592
  11.1 16.1 %collective-permute-start = (bf16[24,1152]{1,0:T(8,128)(2,1)S(1)}, bf16[24,1152]{1,0:T(8,128)(2,1)S(1)}, u32[]{:S(2)}, u32[]{:S(2)}) collective-permute-start(bf16[24,1152]{1,0:T(8,128)(2,1)S(1)} %get-tuple-element.98), channel_id=1, source_target_pairs={{0,1},{1,0},{2,3},{3,2},{4,5},{5,4},{6,7},{7,6},{8,9},{9,8},{10,11... | collective-permute-start | bytes 165896 | tf_op jit(solution)/shard_map/ppermute | solution.py:469
  12.6 9.7 %all-to-all-start = ((f32[8,1,1282]{2,1,0:T(1,128)}), f32[8,1,1282]{2,1,0:T(1,128)S(1)}, u32[]{:S(2)}, u32[]{:S(2)}) async-start(f32[8,1,1282]{2,1,0:T(1,128)} %all_to_all.36), calls=%async_computation | async-start | bytes 90112 | tf_op jit(solution)/shard_map/all_to_all | solution.py:580
  22.7 57.1 %all-to-all-start.1 = ((bf16[16,64,768]{2,1,0:T(8,128)(2,1)}), bf16[16,64,768]{2,1,0:T(8,128)(2,1)S(1)}, u32[]{:S(2)}, u32[]{:S(2)}) async-start(bf16[16,64,768]{2,1,0:T(8,128)(2,1)} %param.19), calls=%async_computation.1 | async-start | bytes 3145728 | tf_op jit(solution)/shard_map/all_to_all | solution.py:569
  27.2 9.9 %collective-permute-start.3 = (bf16[64,1152]{1,0:T(8,128)(2,1)S(1)}, bf16[64,1152]{1,0:T(8,128)(2,1)S(1)}, u32[]{:S(2)}, u32[]{:S(2)}) collective-permute-start(bf16[64,1152]{1,0:T(8,128)(2,1)S(1)} %fusion.29), channel_id=1, source_target_pairs={{0,24},{8,0},{16,8},{24,16},{1,25},{9,1},{17,9},{25,17},{2,26},{10... | collective-permute-start | bytes 442376 | tf_op jit(solution)/shard_map/ppermute | solution.py:474
  30.9 16.7 %collective-permute-start.2 = (bf16[64,1152]{1,0:T(8,128)(2,1)S(1)}, bf16[64,1152]{1,0:T(8,128)(2,1)S(1)}, u32[]{:S(2)}, u32[]{:S(2)}) collective-permute-start(bf16[64,1152]{1,0:T(8,128)(2,1)S(1)} %fusion.29), channel_id=1, source_target_pairs={{0,16},{8,24},{16,0},{24,8},{1,17},{9,25},{17,1},{25,9},{2,18},{10... | collective-permute-start | bytes 442376 | tf_op jit(solution)/shard_map/ppermute | solution.py:474
  30.9 16.7 %collective-permute-start.1 = (bf16[64,1152]{1,0:T(8,128)(2,1)S(1)}, bf16[64,1152]{1,0:T(8,128)(2,1)S(1)}, u32[]{:S(2)}, u32[]{:S(2)}) collective-permute-start(bf16[64,1152]{1,0:T(8,128)(2,1)S(1)} %fusion.29), channel_id=1, source_target_pairs={{0,8},{8,16},{16,24},{24,0},{1,9},{9,17},{17,25},{25,1},{2,10},{10... | collective-permute-start | bytes 442376 | tf_op jit(solution)/shard_map/ppermute | solution.py:474
  47.8 22.4 %collective-permute-start.6 = (bf16[4,48,1152]{2,1,0:T(8,128)(2,1)S(1)}, bf16[4,48,1152]{2,1,0:T(8,128)(2,1)S(1)}, u32[]{:S(2)}, u32[]{:S(2)}) collective-permute-start(bf16[4,48,1152]{2,1,0:T(8,128)(2,1)S(1)} %pad_maximum_fusion.3.refs_0_), channel_id=1, source_target_pairs={{0,6},{1,7},{2,4},{3,5},{4,2},{5,3},{6,0},{7,1},{8,14},{9,15},{10,... | collective-permute-start | bytes 1327112 | tf_op jit(solution)/shard_map/ppermute | solution.py:482
  49.9 28.7 %collective-permute-start.4 = (bf16[4,48,1152]{2,1,0:T(8,128)(2,1)S(1)}, bf16[4,48,1152]{2,1,0:T(8,128)(2,1)S(1)}, u32[]{:S(2)}, u32[]{:S(2)}) collective-permute-start(bf16[4,48,1152]{2,1,0:T(8,128)(2,1)S(1)} %pad_maximum_fusion.3.refs_0_), channel_id=1, source_target_pairs={{0,2},{1,3},{2,0},{3,1},{4,6},{5,7},{6,4},{7,5},{8,10},{9,11},{10,... | collective-permute-start | bytes 1327112 | tf_op jit(solution)/shard_map/ppermute | solution.py:482
  50.8 27.8 %collective-permute-start.5 = (bf16[4,48,1152]{2,1,0:T(8,128)(2,1)S(1)}, bf16[4,48,1152]{2,1,0:T(8,128)(2,1)}, u32[]{:S(2)}, u32[]{:S(2)}) collective-permute-start(bf16[4,48,1152]{2,1,0:T(8,128)(2,1)S(1)} %pad_maximum_fusion.3.refs_0_), channel_id=1, source_target_pairs={{0,4},{1,5},{2,6},{3,7},{4,0},{5,1},{6,2},{7,3},{8,12},{9,13},{10,... | collective-permute-start | bytes 1327112 | tf_op jit(solution)/shard_map/ppermute | solution.py:482
  51.3 29.8 %collective-permute-start.7 = (bf16[4,48,1152]{2,1,0:T(8,128)(2,1)S(1)}, bf16[4,48,1152]{2,1,0:T(8,128)(2,1)}, u32[]{:S(2)}, u32[]{:S(2)}) collective-permute-start(bf16[4,48,1152]{2,1,0:T(8,128)(2,1)S(1)} %pad_maximum_fusion.3.refs_0_), channel_id=1, source_target_pairs={{0,1},{1,0},{2,3},{3,2},{4,5},{5,4},{6,7},{7,6},{8,9},{9,8},{10,11... | collective-permute-start | bytes 1327112 | tf_op jit(solution)/shard_map/ppermute | solution.py:469
  70.2 10.9 %collective-permute-start.10 = (bf16[4,48,1152]{2,1,0:T(8,128)(2,1)S(1)}, bf16[4,48,1152]{2,1,0:T(8,128)(2,1)}, u32[]{:S(2)}, u32[]{:S(2)}) collective-permute-start(bf16[4,48,1152]{2,1,0:T(8,128)(2,1)S(1)} %collective-permute-done.6.refs_3_), channel_id=1, source_target_pairs={{0,1},{1,0},{2,3},{3,2},{4,5},{5,4},{6,7},{7,6},{8,9},{9,8},{10,11... | collective-permute-start | bytes 1327112 | tf_op jit(solution)/shard_map/ppermute | solution.py:469
  106.4 32.5 %all-to-all-start.2 = ((bf16[16,64,768]{2,1,0:T(8,128)(2,1)}), bf16[16,64,768]{2,1,0:T(8,128)(2,1)S(1)}, u32[]{:S(2)}, u32[]{:S(2)}) async-start(bf16[16,64,768]{2,1,0:T(8,128)(2,1)} %tie.16), calls=%async_computation.2 | async-start | bytes 3145728 | tf_op jit(solution)/shard_map/all_to_all | solution.py:623
  168.9 7.0 %collective-permute-start.12 = (bf16[3072,384]{1,0:T(8,128)(2,1)}, bf16[3072,384]{1,0:T(8,128)(2,1)S(1)}, u32[]{:S(2)}, u32[]{:S(2)}) collective-permute-start(bf16[3072,384]{1,0:T(8,128)(2,1)} %convolution_convert_fusion), channel_id=1, source_target_pairs={{0,1},{1,0},{2,3},{3,2},{4,5},{5,4},{6,7},{7,6},{8,9},{9,8},{10,11... | collective-permute-start | bytes 7077896 | tf_op jit(solution)/shard_map/ppermute | solution.py:469
  175.6 12.2 %collective-permute-start.11 = (bf16[768,1536]{1,0:T(8,128)(2,1)}, bf16[768,1536]{1,0:T(8,128)(2,1)}, u32[]{:S(2)}, u32[]{:S(2)}) collective-permute-start(bf16[768,1536]{1,0:T(8,128)(2,1)} %convolution_convert_fusion.1), channel_id=1, source_target_pairs={{0,1},{1,0},{2,3},{3,2},{4,5},{5,4},{6,7},{7,6},{8,9},{9,8},{10,11... | collective-permute-start | bytes 7077896 | tf_op jit(solution)/shard_map/ppermute | solution.py:469
  183.9 33.7 %all-to-all-start.3 = ((bf16[4,4,192,384]{3,2,1,0:T(8,128)(2,1)}), bf16[4,4,192,384]{3,2,1,0:T(8,128)(2,1)S(1)}, u32[]{:S(2)}, u32[]{:S(2)}) async-start(bf16[4,4,192,384]{3,2,1,0:T(8,128)(2,1)} %bitcast.126.refs_10_), calls=%async_computation.3 | async-start | bytes 4718592 | tf_op jit(solution)/shard_map/all_to_all | solution.py:513
  222.1 38.9 %all-to-all-start.4 = ((bf16[4,4,48,1920]{3,2,1,0:T(8,128)(2,1)}), bf16[4,4,48,1920]{3,2,1,0:T(8,128)(2,1)S(1)}, u32[]{:S(2)}, u32[]{:S(2)}) async-start(bf16[4,4,48,1920]{3,2,1,0:T(8,128)(2,1)} %tie.19.refs_5_), calls=%async_computation.4 | async-start | bytes 5898240 | tf_op jit(solution)/shard_map/all_to_all | solution.py:513
  272.8 11.8 %collective-permute-start.15 = (bf16[768,1152]{1,0:T(8,128)(2,1)}, bf16[768,1152]{1,0:T(8,128)(2,1)}, u32[]{:S(2)}, u32[]{:S(2)}) collective-permute-start(bf16[768,1152]{1,0:T(8,128)(2,1)} %convolution_convert_fusion.2), channel_id=1, source_target_pairs={{0,1},{1,0},{2,3},{3,2},{4,5},{5,4},{6,7},{7,6},{8,9},{9,8},{10,11... | collective-permute-start | bytes 5308424 | tf_op jit(solution)/shard_map/ppermute | solution.py:469
  276.2 26.4 %collective-permute-start.24 = (bf16[48,3456]{1,0:T(8,128)(2,1)}, bf16[48,3456]{1,0:T(8,128)(2,1)}, u32[]{:S(2)}, u32[]{:S(2)}) collective-permute-start(bf16[48,3456]{1,0:T(8,128)(2,1)} %get-tuple-element.70.refs_2_), channel_id=1, source_target_pairs={{0,8},{8,16},{16,24},{24,0},{1,9},{9,17},{17,25},{25,1},{2,10},{10... | collective-permute-start | bytes 995336 | tf_op jit(solution)/shard_map/ppermute | solution.py:474
  277.5 25.2 %collective-permute-start.25 = (bf16[48,3456]{1,0:T(8,128)(2,1)}, bf16[48,3456]{1,0:T(8,128)(2,1)}, u32[]{:S(2)}, u32[]{:S(2)}) collective-permute-start(bf16[48,3456]{1,0:T(8,128)(2,1)} %get-tuple-element.71.refs_3_), channel_id=1, source_target_pairs={{0,16},{8,24},{16,0},{24,8},{1,17},{9,25},{17,1},{25,9},{2,18},{10... | collective-permute-start | bytes 995336 | tf_op jit(solution)/shard_map/ppermute | solution.py:474
  278.6 24.2 %collective-permute-start.26 = (bf16[48,3456]{1,0:T(8,128)(2,1)S(1)}, bf16[48,3456]{1,0:T(8,128)(2,1)}, u32[]{:S(2)}, u32[]{:S(2)}) collective-permute-start(bf16[48,3456]{1,0:T(8,128)(2,1)S(1)} %copy-done.14), channel_id=1, source_target_pairs={{0,24},{8,0},{16,8},{24,16},{1,25},{9,1},{17,9},{25,17},{2,26},{10... | collective-permute-start | bytes 995336 | tf_op jit(solution)/shard_map/ppermute | solution.py:474
  280.9 31.5 %all-to-all-start.5 = ((bf16[8,2,64,768]{3,2,1,0:T(8,128)(2,1)}), bf16[8,2,64,768]{3,2,1,0:T(8,128)(2,1)S(1)}, u32[]{:S(2)}, u32[]{:S(2)}) async-start(bf16[8,2,64,768]{3,2,1,0:T(8,128)(2,1)} %tie.21), calls=%async_computation.5 | async-start | bytes 3145728 | tf_op jit(solution)/shard_map/all_to_all | solution.py:572
  290.6 28.2 %collective-permute-start.17 = (bf16[4,56,1152]{2,1,0:T(8,128)(2,1)}, bf16[4,56,1152]{2,1,0:T(8,128)(2,1)}, u32[]{:S(2)}, u32[]{:S(2)}) collective-permute-start(bf16[4,56,1152]{2,1,0:T(8,128)(2,1)} %get-tuple-element.66.refs_4_), channel_id=1, source_target_pairs={{0,2},{1,3},{2,0},{3,1},{4,6},{5,7},{6,4},{7,5},{8,10},{9,11},{10,... | collective-permute-start | bytes 1548296 | tf_op jit(solution)/shard_map/ppermute | solution.py:482
  292.5 26.3 %collective-permute-start.18 = (bf16[4,56,1152]{2,1,0:T(8,128)(2,1)}, bf16[4,56,1152]{2,1,0:T(8,128)(2,1)}, u32[]{:S(2)}, u32[]{:S(2)}) collective-permute-start(bf16[4,56,1152]{2,1,0:T(8,128)(2,1)} %get-tuple-element.65.refs_5_), channel_id=1, source_target_pairs={{0,4},{1,5},{2,6},{3,7},{4,0},{5,1},{6,2},{7,3},{8,12},{9,13},{10,... | collective-permute-start | bytes 1548296 | tf_op jit(solution)/shard_map/ppermute | solution.py:482
  302.6 25.7 %collective-permute-start.19 = (bf16[4,56,1152]{2,1,0:T(8,128)(2,1)}, bf16[4,56,1152]{2,1,0:T(8,128)(2,1)}, u32[]{:S(2)}, u32[]{:S(2)}) collective-permute-start(bf16[4,56,1152]{2,1,0:T(8,128)(2,1)} %get-tuple-element.64.refs_6_), channel_id=1, source_target_pairs={{0,6},{1,7},{2,4},{3,5},{4,2},{5,3},{6,0},{7,1},{8,14},{9,15},{10,... | collective-permute-start | bytes 1548296 | tf_op jit(solution)/shard_map/ppermute | solution.py:482
  308.5 26.3 %collective-permute-start.29 = (f32[96,384]{1,0:T(8,128)}, f32[96,384]{1,0:T(8,128)}, u32[]{:S(2)}, u32[]{:S(2)}) collective-permute-start(f32[96,384]{1,0:T(8,128)} %get-tuple-element.82), channel_id=1, source_target_pairs={{0,1},{1,0},{2,3},{3,2},{4,5},{5,4},{6,7},{7,6},{8,9},{9,8},{10,11... | collective-permute-start | bytes 442376 | tf_op jit(solution)/shard_map/ppermute | solution.py:469
  309.1 8.6 %collective-permute-start.27 = (f32[24,384]{1,0:T(8,128)}, f32[24,384]{1,0:T(8,128)S(1)}, u32[]{:S(2)}, u32[]{:S(2)}) collective-permute-start(f32[24,384]{1,0:T(8,128)} %get-tuple-element.100), channel_id=1, source_target_pairs={{0,1},{1,0},{2,3},{3,2},{4,5},{5,4},{6,7},{7,6},{8,9},{9,8},{10,11... | collective-permute-start | bytes 110600 | tf_op jit(solution)/shard_map/ppermute | solution.py:469
  313.6 31.1 %all-to-all-start.6 = ((bf16[8,2,64,768]{3,2,1,0:T(8,128)(2,1)}), bf16[8,2,64,768]{3,2,1,0:T(8,128)(2,1)S(1)}, u32[]{:S(2)}, u32[]{:S(2)}) async-start(bf16[8,2,64,768]{3,2,1,0:T(8,128)(2,1)} %tie.25), calls=%async_computation.6 | async-start | bytes 3145728 | tf_op jit(solution)/shard_map/all_to_all | solution.py:572
  317.7 16.4 %collective-permute-start.28 = (f32[24,1536]{1,0:T(8,128)}, f32[24,1536]{1,0:T(8,128)S(1)}, u32[]{:S(2)}, u32[]{:S(2)}) collective-permute-start(f32[24,1536]{1,0:T(8,128)} %get-tuple-element.84), channel_id=1, source_target_pairs={{0,1},{1,0},{2,3},{3,2},{4,5},{5,4},{6,7},{7,6},{8,9},{9,8},{10,11... | collective-permute-start | bytes 442376 | tf_op jit(solution)/shard_map/ppermute | solution.py:469
  329.9 8.3 %collective-permute-start.20 = (bf16[56,1152]{1,0:T(8,128)(2,1)S(1)}, bf16[56,1152]{1,0:T(8,128)(2,1)S(1)}, u32[]{:S(2)}, u32[]{:S(2)}) collective-permute-start(bf16[56,1152]{1,0:T(8,128)(2,1)S(1)} %get-tuple-element.78), channel_id=1, source_target_pairs={{0,8},{8,16},{16,24},{24,0},{1,9},{9,17},{17,25},{25,1},{2,10},{10... | collective-permute-start | bytes 387080 | tf_op jit(solution)/shard_map/ppermute | solution.py:474
  330.0 12.0 %collective-permute-start.21 = (bf16[56,1152]{1,0:T(8,128)(2,1)S(1)}, bf16[56,1152]{1,0:T(8,128)(2,1)S(1)}, u32[]{:S(2)}, u32[]{:S(2)}) collective-permute-start(bf16[56,1152]{1,0:T(8,128)(2,1)S(1)} %get-tuple-element.80), channel_id=1, source_target_pairs={{0,16},{8,24},{16,0},{24,8},{1,17},{9,25},{17,1},{25,9},{2,18},{10... | collective-permute-start | bytes 387080 | tf_op jit(solution)/shard_map/ppermute | solution.py:474
  331.3 10.7 %collective-permute-start.22 = (bf16[56,1152]{1,0:T(8,128)(2,1)S(1)}, bf16[56,1152]{1,0:T(8,128)(2,1)S(1)}, u32[]{:S(2)}, u32[]{:S(2)}) collective-permute-start(bf16[56,1152]{1,0:T(8,128)(2,1)S(1)} %get-tuple-element.79), channel_id=1, source_target_pairs={{0,24},{8,0},{16,8},{24,16},{1,25},{9,1},{17,9},{25,17},{2,26},{10... | collective-permute-start | bytes 387080 | tf_op jit(solution)/shard_map/ppermute | solution.py:474
  (50 other events, 295.9 us)
Sparse Core Ops, SparseCore 0:
  11.2 106.6 all-gather.2
